TPU v7x, 32 devices: a whole 2x2x4 slice. The times are simulated.
32 devices in a mesh: dp: 16 (over z, x, core), seq: 2 (over y).
Axes of the slice: x: 2, y: 2, z: 4, core: 2. Of those that a mesh axis runs over, the one named last changes fastest.
Arguments:
- inputs: bfloat16 [16, 258, 1152], P('dp', 'seq'), may hold values from -6 to 6
- skips: bfloat16 [16, 258, 1152], P('dp', None, 'seq'), may hold values from -6 to 6
- cotangent: bfloat16 [16, 258, 1152], P('dp', 'seq'), may hold values from -6 to 6
- bins: int32 [16], P('dp'), may hold values from 0 to 31
- bin_weights: float32 [32], replicated, may hold values from 0.3 to 3
- skip_w: bfloat16 [2304, 1152], P('dp'), may hold values from -0.125 to 0.125
- skip_b: bfloat16 [1152], P('dp'), may hold values from -1 to 1
- ln1_g: bfloat16 [1152], P('dp'), may hold values from 0.5 to 1.5
- ln1_b: bfloat16 [1152], P('dp'), may hold values from -1 to 1
- qkv_w: bfloat16 [1152, 3456], P('dp'), may hold values from -0.25 to 0.25
- proj_w: bfloat16 [1152, 1152], P('dp'), may hold values from -0.75 to 0.75
- proj_b: bfloat16 [1152], P('dp'), may hold values from -1 to 1
- ln2_g: bfloat16 [1152], P('dp'), may hold values from 0.5 to 1.5
- ln2_b: bfloat16 [1152], P('dp'), may hold values from -1 to 1
- fc1_w: bfloat16 [1152, 4608], P('dp'), may hold values from -0.1875 to 0.1875
- fc1_b: bfloat16 [4608], P('dp'), may hold values from -1 to 1
- fc2_w: bfloat16 [4608, 1152], P('dp'), may hold values from -0.125 to 0.125
- fc2_b: bfloat16 [1152], P('dp'), may hold values from -1 to 1
Outputs:
- output: bfloat16 [16, 258, 1152], P('dp', 'seq')
- d_inputs: bfloat16 [16, 258, 1152], P('dp', 'seq')
- d_skips: bfloat16 [16, 258, 1152], P('dp', None, 'seq')
- d_skip_w: float32 [2304, 1152], P('dp')
- d_skip_b: float32 [1152], P('dp')
- d_ln1_g: float32 [1152], P('dp')
- d_ln1_b: float32 [1152], P('dp')
- d_qkv_w: float32 [1152, 3456], P('dp')
- d_proj_w: float32 [1152, 1152], P('dp')
- d_proj_b: float32 [1152], P('dp')
- d_ln2_g: float32 [1152], P('dp')
- d_ln2_b: float32 [1152], P('dp')
- d_fc1_w: float32 [1152, 4608], P('dp')
- d_fc1_b: float32 [4608], P('dp')
- d_fc2_w: float32 [4608, 1152], P('dp')
- d_fc2_b: float32 [1152], P('dp')
All inputs are finite; a program needn't handle non-finite values.
Results may differ from a plain program's by a relative error of at most 0.018.
Values may be sent and summed in bfloat16 or wider, within the bound.
No kernel may reach another device: no remote copies, remote signals or barrier semaphores. Data moves between devices by JAX's collectives and lax.ppermute only.
A program may use at most 256 MiB of HBM per device.

v0:
```python
import jax
import jax.numpy as jnp
from jax import lax
from jax.sharding import PartitionSpec as P

HEADS = 16
HEAD_DIM = 72


def layer_norm(values, gain, shift):
    center = values - jnp.mean(values, axis=-1, keepdims=True)
    spread = jnp.mean(center * center, axis=-1, keepdims=True)
    return center * lax.rsqrt(spread + 1e-05) * gain + shift


def exact_gelu(values):
    return jax.nn.gelu(values, approximate=False)


def matmul(left, right):
    return jnp.dot(left, right, preferred_element_type=jnp.float32)


def left_product(left, right):
    return lax.dot_general(
        left, right, (((0,), (0,)), ((), ())), preferred_element_type=jnp.float32
    )


def right_product(left, right):
    return lax.dot_general(
        left, right, (((1,), (1,)), ((), ())), preferred_element_type=jnp.float32
    )


def token_sum(values):
    return jnp.sum(values.astype(jnp.float32), axis=0)


def body(
    inputs,
    skips,
    cotangent,
    bins,
    bin_weights,
    skip_w,
    skip_b,
    ln1_g,
    ln1_b,
    qkv_w,
    proj_w,
    proj_b,
    ln2_g,
    ln2_b,
    fc1_w,
    fc1_b,
    fc2_w,
    fc2_b,
):
    shards = (
        skip_w,
        skip_b,
        ln1_g,
        ln1_b,
        qkv_w,
        proj_w,
        proj_b,
        ln2_g,
        ln2_b,
        fc1_w,
        fc1_b,
        fc2_w,
        fc2_b,
    )
    full = (
        lax.all_gather(shards[0], "dp", axis=0, tiled=True),
        lax.all_gather(shards[1], "dp", axis=0, tiled=True),
        lax.all_gather(shards[2], "dp", axis=0, tiled=True),
        lax.all_gather(shards[3], "dp", axis=0, tiled=True),
        lax.all_gather(shards[4], "dp", axis=0, tiled=True),
        lax.all_gather(shards[5], "dp", axis=0, tiled=True),
        lax.all_gather(shards[6], "dp", axis=0, tiled=True),
        lax.all_gather(shards[7], "dp", axis=0, tiled=True),
        lax.all_gather(shards[8], "dp", axis=0, tiled=True),
        lax.all_gather(shards[9], "dp", axis=0, tiled=True),
        lax.all_gather(shards[10], "dp", axis=0, tiled=True),
        lax.all_gather(shards[11], "dp", axis=0, tiled=True),
        lax.all_gather(shards[12], "dp", axis=0, tiled=True),
    )
    (
        w_skip,
        b_skip,
        g_one,
        s_one,
        w_qkv,
        w_proj,
        b_proj,
        g_two,
        s_two,
        w_up,
        b_up,
        w_down,
        b_down,
    ) = full
    items, part, width = inputs.shape
    rows = items * part
    factor = HEAD_DIM ** (-0.5)
    local_skip = lax.all_to_all(skips, "seq", split_axis=1, concat_axis=2, tiled=True)
    joined_in = jnp.concatenate((inputs, local_skip), axis=2).reshape(rows, 2 * width)
    hidden = matmul(joined_in, w_skip) + b_skip.astype(jnp.float32)
    normed_f, pull_one = jax.vjp(
        layer_norm, hidden, g_one.astype(jnp.float32), s_one.astype(jnp.float32)
    )
    normed = normed_f.astype(jnp.bfloat16)
    joined = matmul(normed, w_qkv)
    query = joined[:, :width].astype(jnp.bfloat16).reshape(items, part, HEADS, HEAD_DIM)
    keys_here = joined[:, width : 2 * width].astype(jnp.bfloat16).reshape(items, part, width)
    values_here = joined[:, 2 * width :].astype(jnp.bfloat16).reshape(items, part, width)
    keys_all, values_all = (
        lax.all_gather(keys_here, "seq", axis=1, tiled=True),
        lax.all_gather(values_here, "seq", axis=1, tiled=True),
    )
    length = keys_all.shape[1]
    keys = keys_all.reshape(items, length, HEADS, HEAD_DIM)
    values = values_all.reshape(items, length, HEADS, HEAD_DIM)
    scores = jnp.einsum("iqhd,ikhd->ihqk", query, keys, preferred_element_type=jnp.float32) * factor
    top = jnp.max(scores, axis=-1, keepdims=True)
    expo = jnp.exp(scores - top)
    probs_f = expo / jnp.sum(expo, axis=-1, keepdims=True)
    probs = probs_f.astype(jnp.bfloat16)
    mixed = jnp.einsum("ihqk,ikhd->iqhd", probs, values, preferred_element_type=jnp.float32)
    mixed = mixed.reshape(rows, width).astype(jnp.bfloat16)
    middle = hidden + matmul(mixed, w_proj) + b_proj.astype(jnp.float32)
    second_f, pull_two = jax.vjp(
        layer_norm, middle, g_two.astype(jnp.float32), s_two.astype(jnp.float32)
    )
    second = second_f.astype(jnp.bfloat16)
    upper = matmul(second, w_up) + b_up.astype(jnp.float32)
    active_f, pull_gelu = jax.vjp(exact_gelu, upper)
    active = active_f.astype(jnp.bfloat16)
    result = middle + matmul(active, w_down) + b_down.astype(jnp.float32)
    output = result.astype(jnp.bfloat16).reshape(items, part, width)
    picks = bins[:, None] == jnp.arange(bin_weights.shape[0], dtype=jnp.int32)[None, :]
    item_weight = jnp.sum(jnp.where(picks, bin_weights[None, :], 0.0), axis=1)
    grad_out = (cotangent.astype(jnp.float32) * item_weight[:, None, None]).reshape(rows, width)
    d_mlp = grad_out.astype(jnp.bfloat16)
    g_fc2_w = left_product(active, d_mlp)
    g_fc2_b = token_sum(d_mlp)
    d_active = right_product(d_mlp, w_down)
    d_upper = pull_gelu(d_active)[0].astype(jnp.bfloat16)
    g_fc1_w = left_product(second, d_upper)
    g_fc1_b = token_sum(d_upper)
    d_second = right_product(d_upper, w_up)
    d_middle_ln, g_ln2_g, g_ln2_b = pull_two(d_second)
    d_middle = grad_out + d_middle_ln
    d_branch = d_middle.astype(jnp.bfloat16)
    g_proj_w = left_product(mixed, d_branch)
    g_proj_b = token_sum(d_branch)
    d_mixed = (
        right_product(d_branch, w_proj).astype(jnp.bfloat16).reshape(items, part, HEADS, HEAD_DIM)
    )
    d_values = jnp.einsum("ihqk,iqhd->ikhd", probs, d_mixed, preferred_element_type=jnp.float32)
    d_probs = jnp.einsum("iqhd,ikhd->ihqk", d_mixed, values, preferred_element_type=jnp.float32)
    d_scores = probs_f * (d_probs - jnp.sum(d_probs * probs_f, axis=-1, keepdims=True))
    d_scores = d_scores.astype(jnp.bfloat16)
    d_query = (
        jnp.einsum("ihqk,ikhd->iqhd", d_scores, keys, preferred_element_type=jnp.float32) * factor
    )
    d_keys = (
        jnp.einsum("ihqk,iqhd->ikhd", d_scores, query, preferred_element_type=jnp.float32) * factor
    )
    d_keys_here, d_values_here = (
        lax.psum_scatter(
            d_keys.reshape(items, length, width), "seq", scatter_dimension=1, tiled=True
        ),
        lax.psum_scatter(
            d_values.reshape(items, length, width), "seq", scatter_dimension=1, tiled=True
        ),
    )
    d_joined = jnp.concatenate(
        (
            d_query.reshape(rows, width),
            d_keys_here.reshape(rows, width),
            d_values_here.reshape(rows, width),
        ),
        axis=1,
    ).astype(jnp.bfloat16)
    g_qkv_w = left_product(normed, d_joined)
    d_normed = right_product(d_joined, w_qkv)
    d_hidden_ln, g_ln1_g, g_ln1_b = pull_one(d_normed)
    d_hidden = (d_middle + d_hidden_ln).astype(jnp.bfloat16)
    g_skip_w = left_product(joined_in, d_hidden)
    g_skip_b = token_sum(d_hidden)
    d_joined_in = right_product(d_hidden, w_skip)
    d_inputs = d_joined_in[:, :width].astype(jnp.bfloat16).reshape(items, part, width)
    d_skip_here = d_joined_in[:, width:].astype(jnp.bfloat16).reshape(items, part, width)
    d_skips = lax.all_to_all(d_skip_here, "seq", split_axis=2, concat_axis=1, tiled=True)
    summed = (
        lax.psum_scatter(g_skip_w, ("dp", "seq"), scatter_dimension=0, tiled=True),
        lax.psum_scatter(g_skip_b, ("dp", "seq"), scatter_dimension=0, tiled=True),
        lax.psum_scatter(g_ln1_g, ("dp", "seq"), scatter_dimension=0, tiled=True),
        lax.psum_scatter(g_ln1_b, ("dp", "seq"), scatter_dimension=0, tiled=True),
        lax.psum_scatter(g_qkv_w, ("dp", "seq"), scatter_dimension=0, tiled=True),
        lax.psum_scatter(g_proj_w, ("dp", "seq"), scatter_dimension=0, tiled=True),
        lax.psum_scatter(g_proj_b, ("dp", "seq"), scatter_dimension=0, tiled=True),
        lax.psum_scatter(g_ln2_g, ("dp", "seq"), scatter_dimension=0, tiled=True),
        lax.psum_scatter(g_ln2_b, ("dp", "seq"), scatter_dimension=0, tiled=True),
        lax.psum_scatter(g_fc1_w, ("dp", "seq"), scatter_dimension=0, tiled=True),
        lax.psum_scatter(g_fc1_b, ("dp", "seq"), scatter_dimension=0, tiled=True),
        lax.psum_scatter(g_fc2_w, ("dp", "seq"), scatter_dimension=0, tiled=True),
        lax.psum_scatter(g_fc2_b, ("dp", "seq"), scatter_dimension=0, tiled=True),
    )
    final = (
        lax.all_gather(summed[0], "seq", axis=0, tiled=True),
        lax.all_gather(summed[1], "seq", axis=0, tiled=True),
        lax.all_gather(summed[2], "seq", axis=0, tiled=True),
        lax.all_gather(summed[3], "seq", axis=0, tiled=True),
        lax.all_gather(summed[4], "seq", axis=0, tiled=True),
        lax.all_gather(summed[5], "seq", axis=0, tiled=True),
        lax.all_gather(summed[6], "seq", axis=0, tiled=True),
        lax.all_gather(summed[7], "seq", axis=0, tiled=True),
        lax.all_gather(summed[8], "seq", axis=0, tiled=True),
        lax.all_gather(summed[9], "seq", axis=0, tiled=True),
        lax.all_gather(summed[10], "seq", axis=0, tiled=True),
        lax.all_gather(summed[11], "seq", axis=0, tiled=True),
        lax.all_gather(summed[12], "seq", axis=0, tiled=True),
    )
    return (
        output,
        d_inputs,
        d_skips,
        final[0],
        final[1],
        final[2],
        final[3],
        final[4],
        final[5],
        final[6],
        final[7],
        final[8],
        final[9],
        final[10],
        final[11],
        final[12],
    )


def solution(mesh):
    in_specs = (
        P("dp", "seq", None),
        P("dp", None, "seq"),
        P("dp", "seq", None),
        P("dp"),
        P(),
        P("dp", None),
        P("dp"),
        P("dp"),
        P("dp"),
        P("dp", None),
        P("dp", None),
        P("dp"),
        P("dp"),
        P("dp"),
        P("dp", None),
        P("dp"),
        P("dp", None),
        P("dp"),
    )
    out_specs = (
        P("dp", "seq", None),
        P("dp", "seq", None),
        P("dp", None, "seq"),
        P("dp", None),
        P("dp"),
        P("dp"),
        P("dp"),
        P("dp", None),
        P("dp", None),
        P("dp"),
        P("dp"),
        P("dp"),
        P("dp", None),
        P("dp"),
        P("dp", None),
        P("dp"),
    )
    return jax.shard_map(body, mesh=mesh, in_specs=in_specs, out_specs=out_specs, check_vma=False)
```

profile of v0, /device:TPU:0, one launch (start us, length us, event | category | flops | bytes accessed | tf_op | source)
XLA Modules:
  0.0 2381.4 jit_solution(11113093594692177726)
XLA Ops:
  24.1 64.0 %all-reduce.36 = (bf16[1152]{0:T(1024)(128)(2,1)S(1)}, bf16[1152]{0:T(1024)(128)(2,1)S(1)}, bf16[1152]{0:T(1024)(128)(2,1)S(1)}, bf16[1152]{0:T(1024)(128)(2,1)S...) all-reduce(bf16[1152]{0:T(1024)(128)(2,1)S(1)} %dynamic-update-slic, ...), channel_id=1, replica_groups=mesh['dp'=16,'seq'=2] {'dp'}, use_global_device_ids=true, to_apply=%add | all-reduce | flops 12672 | bytes 50688
  97.5 45.4 %all-gather.17.cloned.1.call-done = bf16[1152,3456]{1,0:T(8,128)(2,1)} async-done(((bf16[72,3456]{1,0:T(8,128)(2,1)}), bf16[1152,3456]{1,0:T(8,128)(2,1)}) %all-gather.17.cloned.1.call-update) | async-done | bytes 7962640 | tf_op jit(solution)/shard_map/all_gather | solution.py:80
  147.9 10.2 all-gather.2
  161.7 9.8 all-gather.3
  189.6 86.8 %all-gather.21.cloned.1.call-done = bf16[1152,4608]{1,0:T(8,128)(2,1)} async-done(((bf16[72,4608]{1,0:T(8,128)(2,1)}), bf16[1152,4608]{1,0:T(8,128)(2,1)}) %all-gather.21.cloned.1.call-update) | async-done | bytes 10616848 | tf_op jit(solution)/shard_map/all_gather | solution.py:85
  283.8 13.1 fusion.36
  298.9 66.6 %all-gather.23.cloned.1.call-done = bf16[4608,1152]{1,0:T(8,128)(2,1)} async-done(((bf16[288,1152]{1,0:T(8,128)(2,1)}), bf16[4608,1152]{1,0:T(8,128)(2,1)}) %all-gather.23.cloned.1.call-update) | async-done | bytes 10616848 | tf_op jit(solution)/shard_map/all_gather | solution.py:87
  365.4 12.6 convert_reduce_fusion
  378.0 9.6 multiply_reduce_fusion.2
  418.1 495.4 %all-reduce.39 = (bf16[1,258,1152]{2,0,1:T(2,128)(2,1)}, bf16[1,258,1152]{2,0,1:T(2,128)(2,1)}) all-reduce(f32[1,258,1152]{2,0,1:T(1,128)} %copy.103, f32[1,258,1152]{2,0,1:T(1,128)} %copy.100), channel_id=5, replica_groups=mesh['dp'=16,'seq'=2] {'seq'}, use_global_device_ids=true, to_apply=%region_11.12.clone | all-reduce | flops 594432 | bytes 3566592
  932.3 9.3 fusion.46
  941.6 1073.8 %fusion.55 = (f32[48,3456]{1,0:T(8,128)S(1)}, f32[48,1152]{1,0:T(8,128)}, f32[40,4608]{1,0:T(8,128)S(1)}) fusion(f32[1152,3456]{1,0:T(8,128)} %fusion.31, f32[1152,1152]{1,0:T(8,128)} %fusion.64, f32[1152,4608]{1,0:T(8,128)} %fusion.46), kind=kCustom, calls=%all-reduce-scatter.3 | all-reduce-scatter fusion | flops 12976130 | bytes 44089344
  2015.4 13.4 collective-permute-start.18
  2052.8 17.7 concatenate.11
  2085.4 13.2 collective-permute-start.6
  2131.3 11.2 collective-permute-start.12
  2146.9 10.7 fusion.16
  2157.7 41.4 %all-reduce.33 = (f32[1152]{0:T(1024)S(1)}, f32[1152]{0:T(1024)S(1)}, f32[1152]{0:T(1024)S(1)}, f32[1152]{0:T(1024)S(1)}, f32[1152]{0:T(1024)S(1)}, /*index=5*/f...) all-reduce(f32[1152]{0:T(1024)S(1)} %get-tuple-element.56, ...), channel_id=7, replica_groups=mesh['dp'=16,'seq'=2] {'dp','seq'}, use_global_device_ids=true, to_apply=%region_16.17.clone | all-reduce | flops 12672 | bytes 101376
  2218.2 11.6 collective-permute-start.4
  2242.9 13.7 collective-permute-start.1
  2259.4 18.0 all-reduce.34
  2283.2 14.5 concatenate.10
  2307.3 35.5 %concatenate.9 = f32[420,3456]{1,0:T(8,128)} concatenate(f32[36,3456]{1,0:T(8,128)S(1)} %copy-done.23, f32[48,3456]{1,0:T(8,128)} %collective-permute-done.6, f32[48,3456]{1,0:T(8,128)} %collective-permute-done.5, f32[48,3456]{1,0:T(8,128)} %collective-permute-done.4, f32[48,3456]{1,0:T(8,128)} %collective-permute-done.3, f32[48,3456]{1,0:T(8,128)} %collective-permute-done.2, ...), dimensions={0} | concatenate | bytes 11612160
  2344.0 14.6 all-gather.4
  (323 shorter events, 250.1 us)
Async XLA Ops:
  7.2 86.3 %all-gather.15.cloned.1.call-start = ((), (), s32[]{:S(2)}) async-start(), calls=%async_computation.4 | async-start | bytes 5640192 | tf_op jit(solution)/shard_map/all_gather | solution.py:76
  8.0 135.0 %all-gather.17.cloned.1.call-start = ((), (), s32[]{:S(2)}) async-start(), calls=%async_computation.5 | async-start | bytes 8460288 | tf_op jit(solution)/shard_map/all_gather | solution.py:80
  8.8 178.1 %all-gather.19.cloned.1.call-start = ((), (), s32[]{:S(2)}) async-start(), calls=%async_computation.6 | async-start | bytes 2820096 | tf_op jit(solution)/shard_map/all_gather | solution.py:81
  9.5 266.9 %all-gather.21.cloned.1.call-start = ((), (), s32[]{:S(2)}) async-start(), calls=%async_computation.7 | async-start | bytes 11280384 | tf_op jit(solution)/shard_map/all_gather | solution.py:85
  10.1 355.4 %all-gather.23.cloned.1.call-start = ((), (), s32[]{:S(2)}) async-start(), calls=%async_computation.8 | async-start | bytes 11280384 | tf_op jit(solution)/shard_map/all_gather | solution.py:87
  15.8 73.7 %all-to-all-start = ((bf16[2,2,37152]{2,1,0:T(2,128)(2,1)}), bf16[2,2,37152]{2,1,0:T(2,128)(2,1)S(1)}, u32[]{:S(2)}, u32[]{:S(2)}) async-start(bf16[2,2,37152]{2,1,0:T(2,128)(2,1)} %reshape.339), calls=%async_computation | async-start | bytes 595968 | tf_op jit(solution)/shard_map/all_to_all | solution.py:108
  20.1 2238.9 %reduce-scatter.11.cloned.1.call-start = ((), (), s32[]{:S(2)}) async-start(), calls=%async_computation.9 | async-start | bytes 21897216 | tf_op jit(solution)/shard_map/reduce_scatter | solution.py:210
  297.0 2062.7 %all-gather.27.cloned.1.call-start = ((), (), s32[]{:S(2)}) async-start(), calls=%async_computation.11 | async-start | bytes 2211840 | tf_op jit(solution)/shard_map/all_gather | solution.py:223
  2015.4 29.4 %collective-permute-start.18 = (f32[40,4608]{1,0:T(8,128)S(1)}, f32[40,4608]{1,0:T(8,128)}, u32[]{:S(2)}, u32[]{:S(2)}) collective-permute-start(f32[40,4608]{1,0:T(8,128)S(1)} %get-tuple-element.53), channel_id=1, source_target_pairs={{0,3},{1,4},{2,5},{3,6},{4,7},{5,8},{6,9},{7,10},{8,11},{9,12},{10... | collective-permute-start | bytes 2211848
  2072.5 289.7 %reduce-scatter.13.cloned.1.call-start = ((), (), s32[]{:S(2)}) async-start(), calls=%async_computation.12 | async-start | bytes 10948608
  2085.4 157.5 %collective-permute-start.6 = (f32[48,3456]{1,0:T(8,128)S(1)}, f32[48,3456]{1,0:T(8,128)}, u32[]{:S(2)}, u32[]{:S(2)}) collective-permute-start(f32[48,3456]{1,0:T(8,128)S(1)} %get-tuple-element.51), channel_id=1, source_target_pairs={{0,7},{1,8},{2,9},{3,10},{4,11},{5,12},{6,13},{7,14},{8,15},{9,16}... | collective-permute-start | bytes 1990664
  2098.6 158.0 %collective-permute-start.5 = (f32[48,3456]{1,0:T(8,128)S(1)}, f32[48,3456]{1,0:T(8,128)}, u32[]{:S(2)}, u32[]{:S(2)}) collective-permute-start(f32[48,3456]{1,0:T(8,128)S(1)} %get-tuple-element.51), channel_id=1, source_target_pairs={{0,6},{1,7},{2,8},{3,9},{4,10},{5,11},{6,12},{7,13},{8,14},{9,15},... | collective-permute-start | bytes 1990664
  2101.6 41.0 %collective-permute-start.14 = (f32[48,1152]{1,0:T(8,128)S(1)}, f32[48,1152]{1,0:T(8,128)S(1)}, u32[]{:S(2)}, u32[]{:S(2)}) collective-permute-start(f32[48,1152]{1,0:T(8,128)S(1)} %copy-done.14), channel_id=1, source_target_pairs={{0,7},{1,8},{2,9},{3,10},{4,11},{5,12},{6,13},{7,14},{8,15},{9,16}... | collective-permute-start | bytes 663560
  2105.0 94.1 %collective-permute-start.13 = (f32[48,1152]{1,0:T(8,128)S(1)}, f32[48,1152]{1,0:T(8,128)}, u32[]{:S(2)}, u32[]{:S(2)}) collective-permute-start(f32[48,1152]{1,0:T(8,128)S(1)} %copy-done.14), channel_id=1, source_target_pairs={{0,6},{1,7},{2,8},{3,9},{4,10},{5,11},{6,12},{7,13},{8,14},{9,15},... | collective-permute-start | bytes 663560
  2107.6 23.7 collective-permute-start.15
  2127.7 149.7 %all-to-all-start.1 = ((bf16[2,2,37152]{2,1,0:T(2,128)(2,1)}), bf16[2,2,37152]{2,1,0:T(2,128)(2,1)S(1)}, u32[]{:S(2)}, u32[]{:S(2)}) async-start(bf16[2,2,37152]{2,1,0:T(2,128)(2,1)} %reshape.341), calls=%async_computation.1 | async-start | bytes 595968 | tf_op jit(solution)/shard_map/all_to_all | solution.py:197
  2131.2 240.1 %all-gather.25.cloned.1.call-start = ((), (), s32[]{:S(2)}) async-start(), calls=%async_computation.10 | async-start | bytes 1990656 | tf_op jit(solution)/shard_map/all_gather | solution.py:225
  2131.3 72.0 %collective-permute-start.12 = (f32[48,1152]{1,0:T(8,128)S(1)}, f32[48,1152]{1,0:T(8,128)S(1)}, u32[]{:S(2)}, u32[]{:S(2)}) collective-permute-start(f32[48,1152]{1,0:T(8,128)S(1)} %copy-done.14), channel_id=1, source_target_pairs={{0,5},{1,6},{2,7},{3,8},{4,9},{5,10},{6,11},{7,12},{8,13},{9,14},{... | collective-permute-start | bytes 663560
  2142.5 94.0 %collective-permute-start.7 = (f32[36,3456]{1,0:T(8,128)}, f32[36,3456]{1,0:T(8,128)S(1)}, u32[]{:S(2)}, u32[]{:S(2)}) collective-permute-start(f32[36,3456]{1,0:T(8,128)} %slice.30), channel_id=1, source_target_pairs={{0,8},{1,9},{2,10},{3,11},{4,12},{5,13},{6,14},{7,15},{8,16},{9,17... | collective-permute-start | bytes 1493000
  2218.2 89.1 %collective-permute-start.4 = (f32[48,3456]{1,0:T(8,128)S(1)}, f32[48,3456]{1,0:T(8,128)}, u32[]{:S(2)}, u32[]{:S(2)}) collective-permute-start(f32[48,3456]{1,0:T(8,128)S(1)} %get-tuple-element.51), channel_id=1, source_target_pairs={{0,5},{1,6},{2,7},{3,8},{4,9},{5,10},{6,11},{7,12},{8,13},{9,14},{... | collective-permute-start | bytes 1990664
  2229.8 77.5 %collective-permute-start.3 = (f32[48,3456]{1,0:T(8,128)S(1)}, f32[48,3456]{1,0:T(8,128)}, u32[]{:S(2)}, u32[]{:S(2)}) collective-permute-start(f32[48,3456]{1,0:T(8,128)S(1)} %get-tuple-element.51), channel_id=1, source_target_pairs={{0,4},{1,5},{2,6},{3,7},{4,8},{5,9},{6,10},{7,11},{8,12},{9,13},{1... | collective-permute-start | bytes 1990664
  2236.5 70.8 %collective-permute-start.2 = (f32[48,3456]{1,0:T(8,128)S(1)}, f32[48,3456]{1,0:T(8,128)}, u32[]{:S(2)}, u32[]{:S(2)}) collective-permute-start(f32[48,3456]{1,0:T(8,128)S(1)} %get-tuple-element.51), channel_id=1, source_target_pairs={{0,3},{1,4},{2,5},{3,6},{4,7},{5,8},{6,9},{7,10},{8,11},{9,12},{10... | collective-permute-start | bytes 1990664
  2242.9 64.4 %collective-permute-start.1 = (f32[48,3456]{1,0:T(8,128)S(1)}, f32[48,3456]{1,0:T(8,128)}, u32[]{:S(2)}, u32[]{:S(2)}) collective-permute-start(f32[48,3456]{1,0:T(8,128)S(1)} %get-tuple-element.51), channel_id=1, source_target_pairs={{0,2},{1,3},{2,4},{3,5},{4,6},{5,7},{6,8},{7,9},{8,10},{9,11},{10,... | collective-permute-start | bytes 1990664
  2256.6 50.7 %collective-permute-start = (f32[48,3456]{1,0:T(8,128)S(1)}, f32[48,3456]{1,0:T(8,128)}, u32[]{:S(2)}, u32[]{:S(2)}) collective-permute-start(f32[48,3456]{1,0:T(8,128)S(1)} %get-tuple-element.51), channel_id=1, source_target_pairs={{0,1},{1,2},{2,3},{3,4},{4,5},{5,6},{6,7},{7,8},{8,9},{9,10},{10,1... | collective-permute-start | bytes 1990664
  (76 other events, 2110.1 us)
Sparse Core Ops, SparseCore 0:
  10.2 59.7 all-gather.14
  72.1 70.8 all-gather.16
  145.1 41.6 all-gather.18
  189.0 87.3 all-gather.20
  278.6 86.8 all-gather.22
  371.7 263.5 reduce-scatter.10
  2072.7 33.9 all-gather.26
  2113.7 198.8 reduce-scatter.12
  2314.3 24.1 all-gather.24
where the time goes:
time: 2400 us; the launch traced here: 2380 us
  blocking collectives  1740 us (72%)
  waiting for transfers between devices  212 us (9%)
  local copies, waits for them, and re-layouts  131 us (5%)
  matrix products  128 us (5%)
  starting transfers between devices  127 us (5%)
    unnamed x5, blocking collectives  1690 us
    unnamed x21, starting transfers between devices  119 us
    unnamed x193, local copies, waits for them, and re-layouts  100 us
    all_gather x1, waiting for transfers between devices, body(): lax.all_gather(shards[9], 'dp', axis=0, tiled=True)  86.8 us
    all_gather x1, waiting for transfers between devices, body(): lax.all_gather(shards[11], 'dp', axis=0, tiled=True)  66.6 us
  transfers between devices with their start and end apart: 31, of which 6 were waited for; matrix products, arithmetic and copies ran while one was open for 56% of the time, Pallas kernels for 0%

commit v1 on v0

v1 whole, which is shorter than its diff:
```python
import functools

import jax
import jax.numpy as jnp
from jax import lax
from jax.experimental import pallas as pl
from jax.experimental.pallas import tpu as pltpu
from jax.sharding import Mesh, PartitionSpec as P

HEADS = 16
HEAD_DIM = 72
EPS = 1e-05
F32 = jnp.float32
BF16 = jnp.bfloat16
TEAM = ("near", "core", "seq")
FLIP2 = [(0, 1), (1, 0)]
FLIP4 = [(0, 3), (1, 2), (2, 1), (3, 0)]
VMEM = 56 * 1024 * 1024


def params():
    return pltpu.CompilerParams(vmem_limit_bytes=VMEM)


def nn(a, b):
    return lax.dot_general(a, b, (((1,), (0,)), ((), ())), preferred_element_type=F32)


def nt(a, b):
    return lax.dot_general(a, b, (((1,), (1,)), ((), ())), preferred_element_type=F32)


def tn(a, b):
    return lax.dot_general(a, b, (((0,), (0,)), ((), ())), preferred_element_type=F32)


def norm_forward(total, g, b):
    center = total - jnp.mean(total, axis=-1, keepdims=True)
    spread = jnp.mean(center * center, axis=-1, keepdims=True)
    return center * lax.rsqrt(spread + EPS) * g + b


def norm_kernel(base, a, b, c, d, bias, gain, shift, total_ref, normed_ref):
    total = a[...] + b[...].astype(F32) + c[...].astype(F32) + d[...].astype(F32) + bias[...]
    if base is not None:
        total = total + base[...]
    total_ref[...] = total
    normed_ref[...] = norm_forward(total, gain[...], shift[...]).astype(BF16)


def norm_call(base, parts, bias, gain, shift):
    shape = parts[0].shape
    body = norm_kernel if base is not None else functools.partial(norm_kernel, None)
    ops = (() if base is None else (base,)) + tuple(parts) + (bias, gain, shift)
    return pl.pallas_call(
        body,
        out_shape=(jax.ShapeDtypeStruct(shape, F32), jax.ShapeDtypeStruct(shape, BF16)),
        compiler_params=params(),
        name="norm",
    )(*ops)


def norm_back_kernel(a, b, c, d, total, gain, resid, factor, wide_ref, low_ref, sums_ref):
    grad = a[...] + b[...].astype(F32) + c[...].astype(F32) + d[...].astype(F32)
    center = total[...] - jnp.mean(total[...], axis=-1, keepdims=True)
    spread = jnp.mean(center * center, axis=-1, keepdims=True)
    scale = lax.rsqrt(spread + EPS)
    unit = center * scale
    inner = grad * gain[...]
    back = inner - jnp.mean(inner, axis=-1, keepdims=True)
    back = (back - unit * jnp.mean(inner * unit, axis=-1, keepdims=True)) * scale
    passed = resid[...].astype(F32)
    if factor is not None:
        passed = passed * factor[...]
    wide = passed + back
    low = wide.astype(BF16)
    if wide_ref is not None:
        wide_ref[...] = wide
    low_ref[...] = low
    sums_ref[0:1, :] = jnp.sum(grad * unit, axis=0, keepdims=True)
    sums_ref[1:2, :] = jnp.sum(grad, axis=0, keepdims=True)
    sums_ref[2:3, :] = jnp.sum(low.astype(F32), axis=0, keepdims=True)


def norm_back_first(a, b, c, d, total, gain, resid, factor, wide_ref, low_ref, sums_ref):
    norm_back_kernel(a, b, c, d, total, gain, resid, factor, wide_ref, low_ref, sums_ref)


def norm_back_last(a, b, c, d, total, gain, resid, low_ref, sums_ref):
    norm_back_kernel(a, b, c, d, total, gain, resid, None, None, low_ref, sums_ref)


def norm_back_call(parts, total, gain, resid, factor):
    shape = total.shape
    low = jax.ShapeDtypeStruct(shape, BF16)
    sums = jax.ShapeDtypeStruct((3, shape[1]), F32)
    if factor is None:
        return pl.pallas_call(
            norm_back_last, out_shape=(low, sums), compiler_params=params(), name="norm_back"
        )(*parts, total, gain, resid)
    return pl.pallas_call(
        norm_back_first,
        out_shape=(jax.ShapeDtypeStruct(shape, F32), low, sums),
        compiler_params=params(),
        name="norm_back",
    )(*parts, total, gain, resid, factor)


def key_bias(rows, part):
    place = lax.broadcasted_iota(jnp.int32, (2 * rows, 1), 0)
    place = jnp.where(place >= rows, place - rows, place)
    return jnp.where(place < part, 0.0, -1e30).astype(F32)


def head_masks(width):
    lane = lax.broadcasted_iota(jnp.int32, (1, width), 1)
    return [
        jnp.where((lane >= i * HEAD_DIM) & (lane < (i + 1) * HEAD_DIM), 1.0, 0.0).astype(BF16)
        for i in range(width // HEAD_DIM)
    ]


def probs_of(k, q, bias):
    scores = nt(k, q) * (HEAD_DIM**-0.5) + bias
    expo = jnp.exp(scores - jnp.max(scores, axis=0, keepdims=True))
    return expo / jnp.sum(expo, axis=0, keepdims=True)


def attend_kernel(part, x_ref, qkv_ref, proj_ref, joined_ref, mixed_ref, out_ref):
    joined = nn(x_ref[0], qkv_ref[...]).astype(BF16)
    joined_ref[0] = joined
    width = joined.shape[1] // 3
    q, k, v = (joined[:, i * width : (i + 1) * width] for i in range(3))
    bias = key_bias(joined.shape[0] // 2, part)
    mixed = None
    for mask in head_masks(width):
        probs = probs_of(k, q * mask, bias).astype(BF16)
        term = tn(probs, v * mask)
        mixed = term if mixed is None else mixed + term
    mixed = mixed.astype(BF16)
    mixed_ref[0] = mixed
    out_ref[0] = nn(mixed, proj_ref[...]).astype(out_ref.dtype)


def attend_call(part, x, w_qkv, w_proj, kind):
    items, rows, width = x.shape
    whole = lambda w: pl.BlockSpec(w.shape, lambda i: (0, 0))
    slab = lambda n: pl.BlockSpec((1, rows, n), lambda i: (i, 0, 0))
    inner = w_proj.shape[0]
    return pl.pallas_call(
        functools.partial(attend_kernel, part),
        grid=(items,),
        in_specs=[slab(width), whole(w_qkv), whole(w_proj)],
        out_specs=[slab(3 * inner), slab(inner), slab(width)],
        out_shape=(
            jax.ShapeDtypeStruct((items, rows, 3 * inner), BF16),
            jax.ShapeDtypeStruct((items, rows, inner), BF16),
            jax.ShapeDtypeStruct((items, rows, width), kind),
        ),
        compiler_params=params(),
        name="attend",
    )(x, w_qkv, w_proj)


def attend_back_kernel(part, d_ref, joined_ref, qkv_ref, proj_ref, grads_ref, out_ref):
    d_mixed = nt(d_ref[0], proj_ref[...]).astype(BF16)
    joined = joined_ref[0]
    width = joined.shape[1] // 3
    q, k, v = (joined[:, i * width : (i + 1) * width] for i in range(3))
    bias = key_bias(joined.shape[0] // 2, part)
    d_q = d_k = d_v = 0.0
    for mask in head_masks(width):
        probs = probs_of(k, q * mask, bias)
        d_one = d_mixed * mask
        d_v = d_v + nn(probs.astype(BF16), d_one)
        d_probs = nt(v, d_one)
        inner = jnp.sum(d_probs * probs, axis=0, keepdims=True)
        d_scores = (probs * (d_probs - inner)).astype(BF16)
        d_k = d_k + nn(d_scores, q * mask)
        d_q = d_q + tn(d_scores, k * mask)
    factor = HEAD_DIM**-0.5
    grads = jnp.concatenate((d_q * factor, d_k * factor, d_v), axis=1).astype(BF16)
    grads_ref[0] = grads
    out_ref[0] = nt(grads, qkv_ref[...]).astype(out_ref.dtype)


def attend_back_call(part, d, joined, w_qkv, w_proj, kind):
    items, rows, width = d.shape
    whole = lambda w: pl.BlockSpec(w.shape, lambda i: (0, 0))
    slab = lambda n: pl.BlockSpec((1, rows, n), lambda i: (i, 0, 0))
    return pl.pallas_call(
        functools.partial(attend_back_kernel, part),
        grid=(items,),
        in_specs=[slab(width), slab(joined.shape[2]), whole(w_qkv), whole(w_proj)],
        out_specs=[slab(joined.shape[2]), slab(width)],
        out_shape=(
            jax.ShapeDtypeStruct(joined.shape, BF16),
            jax.ShapeDtypeStruct((items, rows, width), kind),
        ),
        compiler_params=params(),
        name="attend_back",
    )(d, joined, w_qkv, w_proj)


def mlp_kernel(x_ref, d_ref, up_ref, bias_ref, down_ref, act_ref, grad_ref, sum_ref, out_ref, back_ref):
    upper = nn(x_ref[0], up_ref[...]) + bias_ref[...]
    bell = 0.5 * (1.0 + lax.erf(upper * (0.5**0.5)))
    active = (upper * bell).astype(BF16)
    slope = bell + upper * jnp.exp(-0.5 * upper * upper) * 0.3989422804014327
    d_upper = (slope * nt(d_ref[0], down_ref[...])).astype(BF16)
    act_ref[0] = active
    grad_ref[0] = d_upper
    sum_ref[0] = jnp.sum(d_upper.astype(F32), axis=0, keepdims=True)
    back_ref[0] = nt(d_upper, up_ref[...]).astype(back_ref.dtype)
    out_ref[0] = nn(active, down_ref[...]).astype(out_ref.dtype)


def mlp_call(x, d, w_up, b_up, w_down, kind):
    items, rows, width = x.shape
    inner = w_up.shape[1]
    whole = lambda w: pl.BlockSpec(w.shape, lambda i: (0, 0))
    slab = lambda n: pl.BlockSpec((1, rows, n), lambda i: (i, 0, 0))
    return pl.pallas_call(
        mlp_kernel,
        grid=(items,),
        in_specs=[slab(width), slab(width), whole(w_up), whole(b_up), whole(w_down)],
        out_specs=[
            slab(inner),
            slab(inner),
            pl.BlockSpec((1, 1, inner), lambda i: (i, 0, 0)),
            slab(width),
            slab(width),
        ],
        out_shape=(
            jax.ShapeDtypeStruct((items, rows, inner), BF16),
            jax.ShapeDtypeStruct((items, rows, inner), BF16),
            jax.ShapeDtypeStruct((items, 1, inner), F32),
            jax.ShapeDtypeStruct((items, rows, width), kind),
            jax.ShapeDtypeStruct((items, rows, width), kind),
        ),
        compiler_params=params(),
        name="mlp",
    )(x, d, w_up, b_up, w_down)


def swap(v, *axes):
    return lax.ppermute(v, axes if len(axes) > 1 else axes[0], FLIP4 if len(axes) > 1 else FLIP2)


def spread_blocks(own):
    rows, width = own.shape
    quad = jnp.stack(
        (own, swap(own, "seq"), swap(own, "near"), swap(own, "near", "seq"))
    ).reshape(2, 2 * rows, width)
    return quad, swap(quad, "core")


def collect_blocks(mine, theirs, rows):
    width = mine.shape[-1]
    got = swap(theirs, "core")
    total = (mine.astype(F32) + got.astype(F32)).reshape(2, 2, rows, width)
    low = total.astype(BF16)
    return (
        total[0, 0],
        swap(low[0, 1], "seq"),
        swap(low[1, 0], "near"),
        swap(low[1, 1], "near", "seq"),
    )


def relative(blocks, far_first):
    for axis, name in enumerate(TEAM):
        at = {"near": 1, "core": 0, "seq": 2}[name] if far_first else axis
        here = lax.axis_index(name)
        blocks = jnp.where(here == 1, jnp.flip(blocks, axis=at), blocks)
    return blocks


def pad_rows(v, rows, axis):
    pads = [(0, 0)] * v.ndim
    pads[axis] = (0, rows - v.shape[axis])
    return jnp.pad(v, pads)


def gather_far(v):
    return lax.all_gather(v, "far", axis=0, tiled=False)


def pick(v, at, axis):
    return lax.dynamic_index_in_dim(v, at, axis, keepdims=False)


def body(
    inputs,
    skips,
    cotangent,
    bins,
    bin_weights,
    skip_w,
    skip_b,
    ln1_g,
    ln1_b,
    qkv_w,
    proj_w,
    proj_b,
    ln2_g,
    ln2_b,
    fc1_w,
    fc1_b,
    fc2_w,
    fc2_b,
    *,
    far,
):
    _, part, width = inputs.shape
    rows = -(-part // 8) * 8
    team = 8
    dp = far * 4
    hidden_all = fc1_w.shape[1]
    seq = lax.axis_index("seq")
    lo = lax.axis_index("near") * 2 + lax.axis_index("core")
    per = HEADS // team

    deep = width // dp
    k = skip_w.shape[0] // 2
    f = fc2_w.shape[0] // 2
    w_skip = gather_far(pick(skip_w.reshape(2, k, width), seq, 0)).reshape(far * k, width)
    w_down = gather_far(pick(fc2_w.reshape(2, f, width), seq, 0)).reshape(far * f, width)
    qkv_part = pick(qkv_w.reshape(deep, 3, 2, per, 4, HEAD_DIM), seq, 2)
    qkv_part = qkv_part.transpose(3, 0, 1, 2, 4).reshape(4, deep, 3 * per * HEAD_DIM)
    up_part = pick(fc1_w.reshape(deep, far, 4, 2, f), seq, 3)
    up_part = up_part.transpose(2, 0, 1, 3).reshape(4, deep, far * f)
    columns = jnp.concatenate((qkv_part, up_part), axis=2)
    columns = lax.all_to_all(columns, ("near", "core"), split_axis=0, concat_axis=0, tiled=True)
    columns = gather_far(columns).reshape(width, columns.shape[2])
    inner = per * HEAD_DIM
    w_qkv, w_up = columns[:, : 3 * inner], columns[:, 3 * inner :]
    one_head = dp == HEADS
    if one_head:
        w_proj = pick(gather_far(proj_w).reshape(2, per * HEAD_DIM, width), seq, 0)
    else:
        w_proj = lax.all_gather(proj_w, ("far", "near", "core"), axis=0, tiled=True)
        w_proj = pick(w_proj.reshape(2, per, 4, HEAD_DIM, width), seq, 0)
        w_proj = pick(w_proj, lo, 1).reshape(inner, width)
    small = jnp.concatenate((skip_b, ln1_g, ln1_b, proj_b, ln2_g, ln2_b, fc2_b, fc1_b))
    small = lax.all_gather(small, ("far", "near", "core"), axis=0, tiled=False).astype(F32)
    vectors = small[:, : 7 * deep].reshape(dp, 7, deep).transpose(1, 0, 2).reshape(7, 1, width)
    b_skip, g_one, s_one, b_proj, g_two, s_two, b_down = (vectors[i] for i in range(7))
    b_up = small[:, 7 * deep :].reshape(far, 4, 2, f)
    b_up = pick(pick(b_up, lo, 1), seq, 1).reshape(1, far * f)

    picks = bins[:, None] == jnp.arange(bin_weights.shape[0], dtype=jnp.int32)[None, :]
    item_weight = jnp.sum(jnp.where(picks, bin_weights[None, :], 0.0), axis=1)
    factor = jnp.broadcast_to(item_weight.reshape(1, 1), (1, width))
    cot = pad_rows(cotangent[0], rows, 0)
    d_own = (cot.astype(F32) * factor).astype(BF16)
    d_mlp = spread_blocks(d_own)

    half = far // 2
    quarter = far // 4
    x_in = pad_rows(inputs[0], rows, 0).reshape(rows, half, team, k)
    x_in = x_in.transpose(2, 0, 1, 3).reshape(team, rows, half * k)
    x_sk = pad_rows(skips[0].reshape(2, part, -1), rows, 1).reshape(2, rows, quarter, team, k)
    x_sk = x_sk.transpose(3, 1, 0, 2, 4).reshape(team, rows, 2 * quarter * k)
    sent = jnp.concatenate((x_in, x_sk), axis=2)
    got = lax.all_to_all(sent, TEAM, split_axis=0, concat_axis=0, tiled=True)
    got = got.reshape(4, 2, rows, far * k)
    got_sk = got[..., half * k :].reshape(4, 2, rows, 2, quarter * k).transpose(0, 3, 2, 1, 4)
    x_all = jnp.concatenate((got[..., : half * k], got_sk.reshape(4, 2, rows, half * k)), axis=3)
    x_all = x_all.reshape(2, 2, 2, rows, far * k).transpose(1, 0, 2, 3, 4)
    x_all = relative(x_all, True).reshape(2, 4 * rows, far * k)
    theirs = nn(x_all[1], w_skip).astype(BF16).reshape(2, 2 * rows, width)
    mine = nn(x_all[0], w_skip).reshape(2, 2 * rows, width)
    hidden, normed = norm_call(None, collect_blocks(mine, theirs, rows), b_skip, g_one, s_one)

    n1 = spread_blocks(normed)
    joined1, mixed1, theirs = attend_call(part, n1[1], w_qkv, w_proj, BF16)
    joined0, mixed0, mine = attend_call(part, n1[0], w_qkv, w_proj, F32)
    middle, second = norm_call(hidden, collect_blocks(mine, theirs, rows), b_proj, g_two, s_two)

    n2 = spread_blocks(second)
    act1, du1, s1, out1, back1 = mlp_call(n2[1], d_mlp[1], w_up, b_up, w_down, BF16)
    act0, du0, s0, out0, back0 = mlp_call(n2[0], d_mlp[0], w_up, b_up, w_down, F32)
    back = collect_blocks(back0, back1, rows)
    d_middle, d_branch, sums_two = norm_back_call(back, middle, g_two, cot, factor)
    out = collect_blocks(out0, out1, rows)
    output = middle + b_down + out[0]
    for term in out[1:]:
        output = output + term.astype(F32)
    output = output.astype(BF16)[:part].reshape(1, part, width)

    da = spread_blocks(d_branch)
    dj1, theirs = attend_back_call(part, da[1], joined1, w_qkv, w_proj, BF16)
    dj0, mine = attend_back_call(part, da[0], joined0, w_qkv, w_proj, F32)
    back = collect_blocks(mine, theirs, rows)
    d_hidden, sums_one = norm_back_call(back, hidden, g_one, d_middle, None)
    dh = spread_blocks(d_hidden)

    flat = lambda v: v.reshape(-1, v.shape[-1])
    dx1 = nt(flat(dh[1]), w_skip).astype(BF16)
    dx0 = nt(flat(dh[0]), w_skip).astype(BF16)
    dx = jnp.stack((dx0, dx1)).reshape(2, 2, 2, rows, far * k)
    dx = relative(dx, True).transpose(1, 0, 2, 3, 4).reshape(4, 2, rows, far * k)
    dx_sk = dx[..., half * k :].reshape(4, 2, rows, 2, quarter * k).transpose(0, 3, 2, 1, 4)
    sent = jnp.concatenate((dx[..., : half * k], dx_sk.reshape(4, 2, rows, half * k)), axis=3)
    got = lax.all_to_all(
        sent.reshape(team, rows, far * k), TEAM, split_axis=0, concat_axis=0, tiled=True
    )
    d_inputs = got[..., : half * k].reshape(team, rows, half, k).transpose(1, 2, 0, 3)
    d_inputs = d_inputs.reshape(rows, width)[:part].reshape(1, part, width)
    d_skips = got[..., half * k :].reshape(team, rows, 2, quarter, k).transpose(2, 1, 3, 0, 4)
    d_skips = d_skips.reshape(2, rows, width // 2)[:, :part].reshape(1, 2 * part, width // 2)

    def product(left, right):
        return (tn(flat(left[0]), flat(right[0])) + tn(flat(left[1]), flat(right[1]))).astype(BF16)

    g_down = product((act0, act1), d_mlp)
    g_up = product(n2, (du0, du1))
    g_proj = product((mixed0, mixed1), da)
    g_qkv = product(n1, (dj0, dj1))
    g_skip = product((x_all[0], x_all[1]), dh)

    def scatter(v):
        return lax.psum_scatter(v, "far", scatter_dimension=0, tiled=True)

    def both(v):
        return lax.all_gather(v, "seq", axis=0, tiled=False)

    d_fc2_w = both(scatter(g_down)).reshape(2 * f, width).astype(F32)
    d_skip_w = both(scatter(g_skip)).reshape(2 * k, width).astype(F32)
    g_up = scatter(g_up).reshape(4, deep, far * f)
    g_up = both(lax.all_to_all(g_up, ("near", "core"), split_axis=0, concat_axis=0, tiled=True))
    d_fc1_w = g_up.reshape(2, 4, deep, far, f).transpose(2, 3, 1, 0, 4)
    d_fc1_w = d_fc1_w.reshape(deep, hidden_all).astype(F32)
    g_qkv = scatter(g_qkv).reshape(4, deep, 3 * inner)
    g_qkv = both(lax.all_to_all(g_qkv, ("near", "core"), split_axis=0, concat_axis=0, tiled=True))
    d_qkv_w = g_qkv.reshape(2, 4, deep, 3, per, HEAD_DIM).transpose(2, 3, 0, 4, 1, 5)
    d_qkv_w = d_qkv_w.reshape(deep, 3 * width).astype(F32)
    if one_head:
        zero = jnp.zeros_like(g_proj)
        wide = jnp.concatenate(
            (jnp.where(seq == 0, g_proj, zero), jnp.where(seq == 1, g_proj, zero)), axis=0
        )
        low = scatter(wide)
    else:
        wide = jnp.zeros((2, per, 4, HEAD_DIM, width), BF16)
        wide = lax.dynamic_update_slice(
            wide, g_proj.reshape(1, per, 1, HEAD_DIM, width), (seq, 0, lo, 0, 0)
        )
        low = lax.psum_scatter(
            wide.reshape(width, width), ("far", "near", "core"), scatter_dimension=0, tiled=True
        )
    d_proj_w = low.astype(F32) + swap(low, "seq").astype(F32)

    d_down_b = jnp.sum(d_own.astype(F32), axis=0)
    d_up_b = jnp.zeros((far, 4, 2, f), F32)
    d_up_b = lax.dynamic_update_slice(
        d_up_b, (jnp.sum(s0, axis=0) + jnp.sum(s1, axis=0)).reshape(far, 1, 1, f), (0, lo, seq, 0)
    )
    here = jnp.concatenate(
        (
            sums_one[2].reshape(dp, deep),
            sums_one[0].reshape(dp, deep),
            sums_one[1].reshape(dp, deep),
            sums_two[2].reshape(dp, deep),
            sums_two[0].reshape(dp, deep),
            sums_two[1].reshape(dp, deep),
            d_down_b.reshape(dp, deep),
            d_up_b.reshape(dp, 2 * f),
        ),
        axis=1,
    )
    here = lax.psum(here, ("far", "near", "core", "seq"))
    here = pick(here, lax.axis_index("far") * 4 + lo, 0)
    vec = [here[i * deep : (i + 1) * deep] for i in range(7)]

    return (
        output,
        d_inputs,
        d_skips,
        d_skip_w,
        vec[0],
        vec[1],
        vec[2],
        d_qkv_w,
        d_proj_w,
        vec[3],
        vec[4],
        vec[5],
        d_fc1_w,
        here[7 * deep :],
        d_fc2_w,
        vec[6],
    )


def solution(mesh):
    dp, seq = mesh.shape["dp"], mesh.shape["seq"]
    far = dp // 4
    fine = Mesh(mesh.devices.reshape(far, 2, 2, seq), ("far", "near", "core", "seq"))
    items = ("far", "near", "core")
    tokens = P(items, "seq", None)
    features = P(items, None, "seq")
    matrix = P(items, None)
    vector = P(items)
    in_specs = (
        tokens,
        features,
        tokens,
        vector,
        P(),
        matrix,
        vector,
        vector,
        vector,
        matrix,
        matrix,
        vector,
        vector,
        vector,
        matrix,
        vector,
        matrix,
        vector,
    )
    out_specs = (
        tokens,
        tokens,
        features,
        matrix,
        vector,
        vector,
        vector,
        matrix,
        matrix,
        vector,
        vector,
        vector,
        matrix,
        vector,
        matrix,
        vector,
    )
    return jax.shard_map(
        functools.partial(body, far=far),
        mesh=fine,
        in_specs=in_specs,
        out_specs=out_specs,
        check_vma=False,
    )
```

time: 2400 us -> 563 us (0.23)
  blocking collectives: 1740 us -> 195 us
  waiting for transfers between devices: 212 us -> 98.3 us
  matrix products: 128 us -> 38.8 us
  starting transfers between devices: 127 us -> 55.2 us
  local copies, waits for them, and re-layouts: 131 us -> 75.9 us
  Pallas kernels: 0 us -> 55 us
    unnamed x5 -> x1, blocking collectives: 1690 us -> 60.8 us
    all_gather x7 -> x2, waiting for transfers between devices: 199 us -> 0.01 us  [gather_far(): return lax.all_gather(v, 'far', axis=0, tiled=False)]
    unnamed x21 -> x2, starting transfers between devices: 119 us -> 0.33 us
    ppermute x0 -> x41, waiting for transfers between devices: none -> 98.1 us  [swap(): lax.ppermute(v, axes if len(axes) > 1 else axes[0], FLIP4 if len(axes) >...]
    unnamed x193 -> x133, local copies, waits for them, and re-layouts: 100 us -> 5.83 us
    dot_general x21 -> x14, matrix products: 128 us -> 38.8 us  [the longest x10 30.7 us: tn(): lax.dot_general(a, b, (((0,), (0,)), ((), ())), preferred_element_type=F32)]
    pallas_call x0 -> x10, Pallas kernels: none -> 55 us  [the longest x2 16.7 us: mlp_call(): pl.pallas_call(mlp_kernel, grid=(items,), in_specs=[slab(width), slab(wid...]
    psum x0 -> x1, blocking collectives: none -> 44.4 us  [body(): here = lax.psum(here, ('far', 'near', 'core', 'seq'))]
  transfers between devices with their start and end apart: 31 -> 52, of which waited for: 6 -> 24; matrix products, arithmetic and copies ran while one was open for 56% -> 21% of each run, Pallas kernels for 0% -> 7%
where the time goes in v1:
time: 563 us; the launch traced here: 558 us
  blocking collectives  195 us (35%)
  waiting for transfers between devices  98.3 us (17%)
  local copies, waits for them, and re-layouts  75.9 us (13%)
  starting transfers between devices  55.2 us (10%)
  Pallas kernels  55 us (10%)
  matrix products  38.8 us (7%)
  other arithmetic  23 us (4%)
  between operations  17.2 us (3%)
    ppermute x41, waiting for transfers between devices, swap(): lax.ppermute(v, axes if len(axes) > 1 else axes[0], FLIP4 if len(axes) >...  98.1 us
    unnamed x1, blocking collectives  60.8 us
    psum x1, blocking collectives, body(): here = lax.psum(here, ('far', 'near', 'core', 'seq'))  44.4 us
    all_gather x2, blocking collectives, gather_far(): return lax.all_gather(v, 'far', axis=0, tiled=False)  39.9 us
    ppermute x41, starting transfers between devices, swap(): lax.ppermute(v, axes if len(axes) > 1 else axes[0], FLIP4 if len(axes) >...  37.9 us
    all_gather x4, blocking collectives, both(): return lax.all_gather(v, 'seq', axis=0, tiled=False)  36.7 us
    dot_general x10, matrix products, tn(): lax.dot_general(a, b, (((0,), (0,)), ((), ())), preferred_element_type=F32)  30.7 us
    pallas_call x2, Pallas kernels, mlp_call(): pl.pallas_call(mlp_kernel, grid=(items,), in_specs=[slab(width), slab(wid...  16.7 us
  transfers between devices with their start and end apart: 52, of which 24 were waited for; matrix products, arithmetic and copies ran while one was open for 21% of the time, Pallas kernels for 7%

profile of v1, /device:TPU:0, one launch (start us, length us, event | category | flops | bytes accessed | tf_op | source)
XLA Modules:
  0.0 558.2 jit_solution(11880139084939577873)
XLA Ops:
  12.6 5.3 all-to-all-start
  18.0 18.7 %all_gather.50 = bf16[4,72,1152]{2,1,0:T(8,128)(2,1)S(1)} all-gather(bf16[1,72,1152]{2,1,0:T(8,128)(2,1)S(1)} %constant_dynamic-slice_fusion.4), channel_id=1, replica_groups=mesh['far'=4,'near'=2,'core'=2,'seq'=2] {'far'}, dimensions={0}, use_global_device_ids=true | all-gather | bytes 829440 | tf_op jit(solution)/shard_map/all_gather | solution.py:286
  53.7 13.0 %all_to_all.25 = bf16[4,72,1008]{2,1,0:T(8,128)(2,1)} all-to-all(bf16[4,72,1008]{2,1,0:T(8,128)(2,1)S(1)} %pad_maximum_fusion.9), channel_id=1, replica_groups=mesh['far'=4,'near'=2,'core'=2,'seq'=2] {'near','core'}, dimensions={0} | all-to-all | bytes 1161216 | tf_op jit(solution)/shard_map/all_to_all | solution.py:334
  68.4 60.8 %all-reduce.3 = bf16[12672]{0:T(1024)(128)(2,1)S(1)} all-reduce(bf16[12672]{0:T(1024)(128)(2,1)S(1)} %dynamic-update-slice), channel_id=2, replica_groups=mesh['far'=4,'near'=2,'core'=2,'seq'=2] {'far','near','core'}, use_global_device_ids=true, to_apply=%add.3 | all-reduce | flops 12672 | bytes 50688
  139.0 5.2 collective-permute-done.1.b
  164.0 21.3 %all-gather.2 = bf16[288,1152]{1,0:T(8,128)(2,1)S(1)} all-gather(bf16[72,1152]{1,0:T(8,128)(2,1)S(1)} %copy-done.42), channel_id=4, replica_groups=mesh['far'=4,'near'=2,'core'=2,'seq'=2] {'far'}, dimensions={0}, use_global_device_ids=true | all-gather | bytes 829440 | tf_op jit(solution)/shard_map/all_gather | solution.py:286
  189.5 6.1 %attend.3 = (bf16[2,272,432]{2,1,0:T(8,128)(2,1)}, bf16[2,272,144]{2,1,0:T(8,128)(2,1)}, bf16[2,272,1152]{2,1,0:T(8,128)(2,1)}) custom-call(bf16[2,272,1152]{2,1,0:T(8,128)(2,1)} %copy-done.23, bf16[1152,432]{1,0:T(8,128)(2,1)} %slice.280.qkv_ref, bf16[144,1152]{1,0:T(8,128)(2,1)} %dynamic-slice_bitcast_fusion.proj_ref), custom_call_target="tpu_custom_call" | custom-call | tf_op jit(solution)/shard_map/attend/pallas_call | solution.py:150
  196.9 6.4 %attend.2 = (bf16[2,272,432]{2,1,0:T(8,128)(2,1)}, bf16[2,272,144]{2,1,0:T(8,128)(2,1)}, f32[2,272,1152]{2,1,0:T(8,128)}) custom-call(bf16[2,272,1152]{2,1,0:T(8,128)(2,1)} %bitcast.232, bf16[1152,432]{1,0:T(8,128)(2,1)} %slice.280.qkv_ref, bf16[144,1152]{1,0:T(8,128)(2,1)} %dynamic-slice_bitcast_fusion.proj_ref), custom_call_target="tpu_custom_call" | custom-call | tf_op jit(solution)/shard_map/attend/pallas_call | solution.py:150
  220.6 17.4 %collective-permute-done.11.d = bf16[136,1152]{1,0:T(8,128)(2,1)S(1)} collective-permute-done((bf16[136,1152]{1,0:T(8,128)(2,1)}, bf16[136,1152]{1,0:T(8,128)(2,1)S(1)}, u32[]{:S(2)}, u32[]{:S(2)}) %collective-permute-start.11) | collective-permute-done | bytes 313376 | tf_op jit(solution)/shard_map/ppermute | solution.py:247
  265.4 8.1 %mlp.3 = (bf16[2,272,576]{2,1,0:T(8,128)(2,1)}, bf16[2,272,576]{2,1,0:T(8,128)(2,1)}, f32[2,1,576]{2,1,0:T(1,128)}, bf16[2,272,1152]{2,1,0:T(8,128)(2,1)}, bf16[2,272,1152]{2,1,0:T(8,128)(2,1)}) custom-call(bf16[2,272,1152]{2,1,0:T(8,128)(2,1)} %collective-permute-done.18.x_ref, bf16[2,272,1152]{2,1,0:T(8,128)(2,1)} %collective-permute-done.19.d_ref, ...), custom_call_target="tpu_custom_call" | custom-call | tf_op jit(solution)/shard_map/mlp/pallas_call | solution.py:223
  274.8 8.6 %mlp.2 = (bf16[2,272,576]{2,1,0:T(8,128)(2,1)}, bf16[2,272,576]{2,1,0:T(8,128)(2,1)}, f32[2,1,576]{2,1,0:T(1,128)}, f32[2,272,1152]{2,1,0:T(8,128)}, f32[2,272,1152]{2,1,0:T(8,128)}) custom-call(bf16[2,272,1152]{2,1,0:T(8,128)(2,1)} %bitcast.229, bf16[2,272,1152]{2,1,0:T(8,128)(2,1)} %bitcast.226, bf16[1152,576]{1,0:T(8,128)(2,1)} %slice.289.up_ref, ...), custom_call_target="tpu_custom_call" | custom-call | tf_op jit(solution)/shard_map/mlp/pallas_call | solution.py:223
  302.0 5.4 collective-permute-done.25.b
  308.5 6.8 %collective-permute-done.27.d = bf16[136,1152]{1,0:T(8,128)(2,1)S(1)} collective-permute-done((bf16[136,1152]{1,0:T(8,128)(2,1)S(1)}, bf16[136,1152]{1,0:T(8,128)(2,1)S(1)}, u32[]{:S(2)}, u32[]{:S(2)}) %collective-permute-start.27) | collective-permute-done | bytes 313376 | tf_op jit(solution)/shard_map/ppermute | solution.py:247
  331.1 5.9 %collective-permute-done.30 = bf16[136,1152]{1,0:T(8,128)(2,1)} collective-permute-done((bf16[136,1152]{1,0:T(8,128)(2,1)}, bf16[136,1152]{1,0:T(8,128)(2,1)}, u32[]{:S(2)}, u32[]{:S(2)}) %collective-permute-start.30) | collective-permute-done | bytes 313376 | tf_op jit(solution)/shard_map/ppermute | solution.py:247
  342.5 6.8 %attend_back.3 = (bf16[2,272,432]{2,1,0:T(8,128)(2,1)}, bf16[2,272,1152]{2,1,0:T(8,128)(2,1)}) custom-call(bf16[2,272,1152]{2,1,0:T(8,128)(2,1)} %collective-permute-done.31.d_ref, bf16[2,272,432]{2,1,0:T(8,128)(2,1)} %get-tuple-element.58.joined_ref, bf16[1152,432]{1,0:T(8,128)(2,1)} %slice.280.qkv_ref, bf16[144,1152]{1,0:T(8,128)(2,1)} %dynamic-slice_bitcast_fusion.proj_ref), custom_call_target="tpu_custom_call" | custom-call | tf_op jit(solution)/shard_map/attend_back/pallas_call | solution.py:191
  352.3 7.1 %attend_back.2 = (bf16[2,272,432]{2,1,0:T(8,128)(2,1)}, f32[2,272,1152]{2,1,0:T(8,128)}) custom-call(bf16[2,272,1152]{2,1,0:T(8,128)(2,1)} %bitcast.70.d_ref, bf16[2,272,432]{2,1,0:T(8,128)(2,1)} %get-tuple-element.56.joined_ref, bf16[1152,432]{1,0:T(8,128)(2,1)} %slice.280.qkv_ref, bf16[144,1152]{1,0:T(8,128)(2,1)} %dynamic-slice_bitcast_fusion.proj_ref), custom_call_target="tpu_custom_call" | custom-call | tf_op jit(solution)/shard_map/attend_back/pallas_call | solution.py:191
  374.6 5.1 collective-permute-done.33.b
  381.9 6.8 %collective-permute-done.35.d = bf16[136,1152]{1,0:T(8,128)(2,1)S(1)} collective-permute-done((bf16[136,1152]{1,0:T(8,128)(2,1)S(1)}, bf16[136,1152]{1,0:T(8,128)(2,1)S(1)}, u32[]{:S(2)}, u32[]{:S(2)}) %collective-permute-start.35) | collective-permute-done | bytes 313376 | tf_op jit(solution)/shard_map/ppermute | solution.py:247
  402.2 6.1 %collective-permute-done.37 = bf16[136,1152]{1,0:T(8,128)(2,1)S(1)} collective-permute-done((bf16[136,1152]{1,0:T(8,128)(2,1)S(1)}, bf16[136,1152]{1,0:T(8,128)(2,1)S(1)}, u32[]{:S(2)}, u32[]{:S(2)}) %collective-permute-start.37) | collective-permute-done | bytes 313376 | tf_op jit(solution)/shard_map/ppermute | solution.py:247
  419.8 11.1 %all-gather.6 = bf16[288,1152]{1,0:T(8,128)(2,1)S(1)} all-gather(bf16[144,1152]{1,0:T(8,128)(2,1)} %reduce-scatter.14.cloned.1.call-done), channel_id=8, replica_groups=mesh['far'=4,'near'=2,'core'=2,'seq'=2] {'seq'}, dimensions={0}, use_global_device_ids=true | all-gather | bytes 995328 | tf_op jit(solution)/shard_map/all_gather | solution.py:427
  432.1 10.9 %all-gather.5 = bf16[8,72,576]{2,1,0:T(8,128)(2,1)S(1)} all-gather(bf16[4,72,576]{2,1,0:T(8,128)(2,1)S(1)} %all-to-all-done.4), channel_id=7, replica_groups=mesh['far'=4,'near'=2,'core'=2,'seq'=2] {'seq'}, dimensions={0}, use_global_device_ids=true | all-gather | bytes 995328 | tf_op jit(solution)/shard_map/all_gather | solution.py:427
  477.8 44.4 %psum.7 = f32[16,792]{1,0:T(8,128)S(1)} all-reduce(f32[16,792]{1,0:T(8,128)S(1)} %concatenate.41), channel_id=1, replica_groups=mesh['far'=4,'near'=2,'core'=2,'seq'=2] {'far','near','core','seq'}, use_global_device_ids=true, to_apply=%region_5.6 | all-reduce | flops 12672 | bytes 101376 | tf_op jit(solution)/shard_map/psum | solution.py:473
  523.5 8.6 %all-gather.4 = bf16[8,72,432]{2,1,0:T(8,128)(2,1)S(1)} all-gather(bf16[4,72,432]{2,1,0:T(8,128)(2,1)S(1)} %all-to-all-done.3), channel_id=6, replica_groups=mesh['far'=4,'near'=2,'core'=2,'seq'=2] {'seq'}, dimensions={0}, use_global_device_ids=true | all-gather | bytes 746496 | tf_op jit(solution)/shard_map/all_gather | solution.py:427
  543.8 6.2 %all-gather.3 = bf16[144,1152]{1,0:T(8,128)(2,1)S(1)} all-gather(bf16[72,1152]{1,0:T(8,128)(2,1)} %reduce-scatter.16.cloned.1.call-done), channel_id=5, replica_groups=mesh['far'=4,'near'=2,'core'=2,'seq'=2] {'seq'}, dimensions={0}, use_global_device_ids=true | all-gather | bytes 497664 | tf_op jit(solution)/shard_map/all_gather | solution.py:427
  (380 shorter events, 239.1 us)
Async XLA Ops:
  12.6 24.1 %all-to-all-start = ((bf16[8,136,288]{2,1,0:T(8,128)(2,1)}), bf16[8,136,288]{2,1,0:T(8,128)(2,1)S(1)}, u32[]{:S(2)}, u32[]{:S(2)}) async-start(bf16[8,136,288]{2,1,0:T(8,128)(2,1)} %copy.74), calls=%async_computation | async-start | bytes 1671168 | tf_op jit(solution)/shard_map/all_to_all | solution.py:366
  17.9 168.2 %all-gather.12.cloned.1.call-start = ((), (), s32[]{:S(2)}) async-start(), calls=%async_computation.14 | async-start | bytes 2949120 | tf_op jit(solution)/shard_map/all_gather | solution.py:286
  40.4 91.8 %collective-permute-start = (bf16[2,272,1152]{2,1,0:T(8,128)(2,1)}, bf16[2,272,1152]{2,1,0:T(8,128)(2,1)}, u32[]{:S(2)}, u32[]{:S(2)}) collective-permute-start(bf16[2,272,1152]{2,1,0:T(8,128)(2,1)} %bitcast.16), channel_id=1, source_target_pairs={{0,2},{2,0},{1,3},{3,1},{4,6},{6,4},{5,7},{7,5},{8,10},{10,8},{9,1... | collective-permute-start | bytes 3760136 | tf_op jit(solution)/shard_map/ppermute | solution.py:247
  66.7 198.7 %all-gather.10.cloned.1.call-start = ((), (), s32[]{:S(2)}) async-start(), calls=%async_computation.10 | async-start | bytes 1658880 | tf_op jit(solution)/shard_map/all_gather | solution.py:286
  163.9 24.5 %collective-permute-start.7 = (bf16[2,272,1152]{2,1,0:T(8,128)(2,1)S(1)}, bf16[2,272,1152]{2,1,0:T(8,128)(2,1)S(1)}, u32[]{:S(2)}, u32[]{:S(2)}) collective-permute-start(bf16[2,272,1152]{2,1,0:T(8,128)(2,1)S(1)} %bitcast.231), channel_id=1, source_target_pairs={{0,2},{2,0},{1,3},{3,1},{4,6},{6,4},{5,7},{7,5},{8,10},{10,8},{9,1... | collective-permute-start | bytes 3760136 | tf_op jit(solution)/shard_map/ppermute | solution.py:247
  208.6 38.4 %collective-permute-start.15 = (bf16[136,1152]{1,0:T(8,128)(2,1)S(1)}, bf16[136,1152]{1,0:T(8,128)(2,1)}, u32[]{:S(2)}, u32[]{:S(2)}) collective-permute-start(bf16[136,1152]{1,0:T(8,128)(2,1)S(1)} %get-tuple-element.88), channel_id=1, source_target_pairs={{0,1},{1,0},{2,3},{3,2},{4,5},{5,4},{6,7},{7,6},{8,9},{9,8},{10,11... | collective-permute-start | bytes 940040 | tf_op jit(solution)/shard_map/ppermute | solution.py:247
  210.8 37.7 %collective-permute-start.16 = (bf16[136,1152]{1,0:T(8,128)(2,1)S(1)}, bf16[136,1152]{1,0:T(8,128)(2,1)}, u32[]{:S(2)}, u32[]{:S(2)}) collective-permute-start(bf16[136,1152]{1,0:T(8,128)(2,1)S(1)} %get-tuple-element.88), channel_id=1, source_target_pairs={{0,4},{4,0},{1,5},{5,1},{2,6},{6,2},{3,7},{7,3},{8,12},{12,8},{9,1... | collective-permute-start | bytes 940040 | tf_op jit(solution)/shard_map/ppermute | solution.py:247
  210.9 37.6 %collective-permute-start.17 = (bf16[136,1152]{1,0:T(8,128)(2,1)S(1)}, bf16[136,1152]{1,0:T(8,128)(2,1)}, u32[]{:S(2)}, u32[]{:S(2)}) collective-permute-start(bf16[136,1152]{1,0:T(8,128)(2,1)S(1)} %get-tuple-element.88), channel_id=1, source_target_pairs={{0,5},{1,4},{4,1},{5,0},{2,7},{3,6},{6,3},{7,2},{8,13},{9,12},{12,... | collective-permute-start | bytes 940040 | tf_op jit(solution)/shard_map/ppermute | solution.py:247
  213.1 202.9 %reduce-scatter.12.cloned.1.call-start = ((), (), s32[]{:S(2)}) async-start(), calls=%async_computation.12 | async-start | bytes 1843200 | tf_op jit(solution)/shard_map/reduce_scatter | solution.py:424
  217.8 20.2 %collective-permute-start.11 = (bf16[136,1152]{1,0:T(8,128)(2,1)}, bf16[136,1152]{1,0:T(8,128)(2,1)S(1)}, u32[]{:S(2)}, u32[]{:S(2)}) collective-permute-start(bf16[136,1152]{1,0:T(8,128)(2,1)} %get-tuple-element.98), channel_id=1, source_target_pairs={{0,5},{1,4},{4,1},{5,0},{2,7},{3,6},{6,3},{7,2},{8,13},{9,12},{12,... | collective-permute-start | bytes 940040 | tf_op jit(solution)/shard_map/ppermute | solution.py:247
  219.2 22.3 %collective-permute-start.9 = (bf16[136,1152]{1,0:T(8,128)(2,1)}, bf16[136,1152]{1,0:T(8,128)(2,1)S(1)}, u32[]{:S(2)}, u32[]{:S(2)}) collective-permute-start(bf16[136,1152]{1,0:T(8,128)(2,1)} %get-tuple-element.100), channel_id=1, source_target_pairs={{0,1},{1,0},{2,3},{3,2},{4,5},{5,4},{6,7},{7,6},{8,9},{9,8},{10,11... | collective-permute-start | bytes 940040 | tf_op jit(solution)/shard_map/ppermute | solution.py:247
  273.5 20.3 %collective-permute-start.20 = (bf16[2,272,1152]{2,1,0:T(8,128)(2,1)}, bf16[2,272,1152]{2,1,0:T(8,128)(2,1)S(1)}, u32[]{:S(2)}, u32[]{:S(2)}) collective-permute-start(bf16[2,272,1152]{2,1,0:T(8,128)(2,1)} %get-tuple-element.52), channel_id=1, source_target_pairs={{0,2},{2,0},{1,3},{3,1},{4,6},{6,4},{5,7},{7,5},{8,10},{10,8},{9,1... | collective-permute-start | bytes 3760136 | tf_op jit(solution)/shard_map/ppermute | solution.py:247
  274.0 19.8 %collective-permute-start.24 = (bf16[2,272,1152]{2,1,0:T(8,128)(2,1)}, bf16[2,272,1152]{2,1,0:T(8,128)(2,1)S(1)}, u32[]{:S(2)}, u32[]{:S(2)}) collective-permute-start(bf16[2,272,1152]{2,1,0:T(8,128)(2,1)} %get-tuple-element.54), channel_id=1, source_target_pairs={{0,2},{2,0},{1,3},{3,1},{4,6},{6,4},{5,7},{7,5},{8,10},{10,8},{9,1... | collective-permute-start | bytes 3760136 | tf_op jit(solution)/shard_map/ppermute | solution.py:247
  289.1 130.7 %reduce-scatter.14.cloned.1.call-start = ((), (), s32[]{:S(2)}) async-start(), calls=%async_computation.13 | async-start | bytes 1658880 | tf_op jit(solution)/shard_map/reduce_scatter | solution.py:424
  327.6 126.4 %reduce-scatter.18.cloned.1.call-start = ((), (), s32[]{:S(2)}) async-start(), calls=%async_computation.16 | async-start | bytes 829440
  349.3 19.0 %collective-permute-start.32 = (bf16[2,272,1152]{2,1,0:T(8,128)(2,1)}, bf16[2,272,1152]{2,1,0:T(8,128)(2,1)}, u32[]{:S(2)}, u32[]{:S(2)}) collective-permute-start(bf16[2,272,1152]{2,1,0:T(8,128)(2,1)} %get-tuple-element.59), channel_id=1, source_target_pairs={{0,2},{2,0},{1,3},{3,1},{4,6},{6,4},{5,7},{7,5},{8,10},{10,8},{9,1... | collective-permute-start | bytes 3760136 | tf_op jit(solution)/shard_map/ppermute | solution.py:247
  350.4 63.5 %collective-permute-start.21 = (bf16[136,1152]{1,0:T(8,128)(2,1)}, bf16[136,1152]{1,0:T(8,128)(2,1)}, u32[]{:S(2)}, u32[]{:S(2)}) collective-permute-start(bf16[136,1152]{1,0:T(8,128)(2,1)} %get-tuple-element.95), channel_id=1, source_target_pairs={{0,1},{1,0},{2,3},{3,2},{4,5},{5,4},{6,7},{7,6},{8,9},{9,8},{10,11... | collective-permute-start | bytes 940040 | tf_op jit(solution)/shard_map/ppermute | solution.py:247
  350.7 63.2 %collective-permute-start.22 = (bf16[136,1152]{1,0:T(8,128)(2,1)}, bf16[136,1152]{1,0:T(8,128)(2,1)}, u32[]{:S(2)}, u32[]{:S(2)}) collective-permute-start(bf16[136,1152]{1,0:T(8,128)(2,1)} %get-tuple-element.97), channel_id=1, source_target_pairs={{0,4},{4,0},{1,5},{5,1},{2,6},{6,2},{3,7},{7,3},{8,12},{12,8},{9,1... | collective-permute-start | bytes 940040 | tf_op jit(solution)/shard_map/ppermute | solution.py:247
  364.0 94.0 %reduce-scatter.10.cloned.1.call-start = ((), (), s32[]{:S(2)}) async-start(), calls=%async_computation.11 | async-start | bytes 1474560 | tf_op jit(solution)/shard_map/reduce_scatter | solution.py:424
  379.7 34.3 %collective-permute-start.23 = (bf16[136,1152]{1,0:T(8,128)(2,1)S(1)}, bf16[136,1152]{1,0:T(8,128)(2,1)}, u32[]{:S(2)}, u32[]{:S(2)}) collective-permute-start(bf16[136,1152]{1,0:T(8,128)(2,1)S(1)} %get-tuple-element.96), channel_id=1, source_target_pairs={{0,5},{1,4},{4,1},{5,0},{2,7},{3,6},{6,3},{7,2},{8,13},{9,12},{12,... | collective-permute-start | bytes 940040 | tf_op jit(solution)/shard_map/ppermute | solution.py:247
  413.9 47.9 %collective-permute-start.39 = (bf16[2,272,1152]{2,1,0:T(8,128)(2,1)}, bf16[2,272,1152]{2,1,0:T(8,128)(2,1)}, u32[]{:S(2)}, u32[]{:S(2)}) collective-permute-start(bf16[2,272,1152]{2,1,0:T(8,128)(2,1)} %bitcast.83), channel_id=1, source_target_pairs={{0,2},{2,0},{1,3},{3,1},{4,6},{6,4},{5,7},{7,5},{8,10},{10,8},{9,1... | collective-permute-start | bytes 3760136 | tf_op jit(solution)/shard_map/ppermute | solution.py:247
  454.0 22.6 %collective-permute-start.40 = (bf16[72,1152]{1,0:T(8,128)(2,1)}, bf16[72,1152]{1,0:T(8,128)(2,1)S(1)}, u32[]{:S(2)}, u32[]{:S(2)}) collective-permute-start(bf16[72,1152]{1,0:T(8,128)(2,1)} %reduce-scatter.18.cloned.1.call-done), channel_id=1, source_target_pairs={{0,1},{1,0},{2,3},{3,2},{4,5},{5,4},{6,7},{7,6},{8,9},{9,8},{10,11... | collective-permute-start | bytes 497672 | tf_op jit(solution)/shard_map/ppermute | solution.py:247
  461.4 82.4 %reduce-scatter.16.cloned.1.call-start = ((), (), s32[]{:S(2)}) async-start(), calls=%async_computation.15 | async-start | bytes 829440
  472.9 66.5 %all-to-all-start.2 = ((bf16[8,136,288]{2,1,0:T(8,128)(2,1)}), bf16[8,136,288]{2,1,0:T(8,128)(2,1)S(1)}, u32[]{:S(2)}, u32[]{:S(2)}) async-start(bf16[8,136,288]{2,1,0:T(8,128)(2,1)} %copy.88), calls=%async_computation.2 | async-start | bytes 1671168 | tf_op jit(solution)/shard_map/all_to_all | solution.py:406
  (93 other events, 1089.7 us)
Sparse Core Ops, SparseCore 0:
  66.8 50.1 all-gather.11
  213.2 32.5 all-gather.9
  289.3 32.8 reduce-scatter.11
  327.8 30.9 reduce-scatter.13
  364.1 21.9 reduce-scatter.17
  398.1 27.7 reduce-scatter.9
  469.1 22.5 reduce-scatter.15

commit v2 on v1

v2 whole, which is shorter than its diff:
```python
import functools

import jax
import jax.numpy as jnp
from jax import lax
from jax.experimental import pallas as pl
from jax.experimental.pallas import tpu as pltpu
from jax.sharding import Mesh, PartitionSpec as P

HEADS = 16
HEAD_DIM = 72
EPS = 1e-05
F32 = jnp.float32
BF16 = jnp.bfloat16
TEAM = ("near", "core", "seq")
LITTLE, WINDOW, FIRST = 5, 20, 100
FLIP2 = [(0, 1), (1, 0)]
FLIP4 = [(0, 3), (1, 2), (2, 1), (3, 0)]


def nn(a, b):
    return lax.dot_general(a, b, (((1,), (0,)), ((), ())), preferred_element_type=F32)


def nt(a, b):
    return lax.dot_general(a, b, (((1,), (1,)), ((), ())), preferred_element_type=F32)


def tn(a, b):
    return lax.dot_general(a, b, (((0,), (0,)), ((), ())), preferred_element_type=F32)


def shape(dims, kind):
    return jax.ShapeDtypeStruct(tuple(dims), kind)


class Line:
    def __init__(self):
        self.word = None

    def __call__(self, kernel, outs, *ops, scratch=(), limit=12, name=None, scalars=(), cost=0.1):
        single = not isinstance(outs, tuple)
        outs = (outs,) if single else outs
        spec = pl.BlockSpec(memory_space=pltpu.VMEM)
        n, m = len(ops) + len(scalars), len(outs)
        late = () if self.word is None else (self.word,)

        def call(*refs):
            ins, rest = refs[:n], refs[n + len(late) :]
            rest[m][...] = jnp.zeros_like(rest[m])
            kernel(*ins, *rest[:m], *rest[m + 1 :])

        *results, self.word = pl.pallas_call(
            call,
            out_shape=outs + (jax.ShapeDtypeStruct((8, 128), F32),),
            in_specs=[spec] * len(ops)
            + [pl.BlockSpec(memory_space=pltpu.SMEM)] * len(scalars)
            + [pl.BlockSpec(memory_space=pl.ANY)] * len(late),
            out_specs=(spec,) * (m + 1),
            scratch_shapes=list(scratch),
            cost_estimate=pl.CostEstimate(flops=int(cost * 1e9), bytes_accessed=1000, transcendentals=0),
            compiler_params=pltpu.CompilerParams(vmem_limit_bytes=limit * 1024 * 1024),
            name=name,
        )(*ops, *scalars, *late)
        return results[0] if single else tuple(results)


def pack_kernel(half, quarter, k, x_ref, s_ref, out_ref, wide, tall):
    part = x_ref.shape[0]
    x = x_ref[...].astype(F32)
    wide[0 : 2 * part, :] = s_ref[...].astype(F32)
    first, second = wide[0:part, :], wide[part : 2 * part, :]
    tall[part:, :] = jnp.zeros((tall.shape[0] - part, tall.shape[1]), F32)
    for r in range(8):
        pieces = [
            src[:, (j * 8 + r) * k : (j * 8 + r + 1) * k]
            for src, n in ((x, half), (first, quarter), (second, quarter))
            for j in range(n)
        ]
        tall[0:part, :] = jnp.concatenate(pieces, axis=1)
        out_ref[r] = tall[...].astype(BF16)


def pack_call(run, x, s, rows, half, quarter, k):
    deep = 2 * half * k
    return run(
        functools.partial(pack_kernel, half, quarter, k),
        shape((8, rows, deep), BF16),
        x,
        s,
        scratch=[pltpu.VMEM((s.shape[0], s.shape[1]), F32), pltpu.VMEM((rows, deep), F32)],
        name="pack",
        cost=FIRST,
    )


def skip_half_kernel(w_ref, *refs):
    *small, out_ref = refs
    k = w_ref.shape[0] // 2
    w = w_ref[...].astype(F32)
    w = jnp.where(lax.axis_index("seq") == 0, w[:k], w[k:])
    line = [ref[...].astype(F32) for ref in small]
    line.append(jnp.zeros((1, w.shape[1] - sum(v.shape[1] for v in line)), F32))
    line = jnp.concatenate(line, axis=1)
    line = jnp.where(lax.broadcasted_iota(jnp.int32, (8, 1), 0) == 0, line, 0.0)
    out_ref[...] = jnp.concatenate((w, line), axis=0).astype(BF16)


def lo_index():
    return lax.axis_index("near") * 2 + lax.axis_index("core")


def choose(at, values):
    out = values[0]
    for i in range(1, len(values)):
        out = jnp.where(at == i, values[i], out)
    return out


def pack_columns_kernel(far, per, joint, f, qkv_ref, up_ref, *outs):
    seq = lax.axis_index("seq")
    lo = lo_index()
    w, up = qkv_ref[...].astype(F32), up_ref[...].astype(F32)
    deep, width = w.shape[0], w.shape[1] // 3
    spare = jnp.zeros((deep, joint - 3 * per * HEAD_DIM), F32)
    blocks = []
    for j in range(4):
        both = []
        for s in range(2):
            heads = [
                w[:, at : at + HEAD_DIM]
                for b in range(3)
                for i in range(per)
                for at in (b * width + ((s * per + i) * 4 + j) * HEAD_DIM,)
            ]
            hidden = [up[:, at : at + f] for z in range(far) for at in (((z * 4 + j) * 2 + s) * f,)]
            both.append(jnp.concatenate(heads + [spare] + hidden, axis=1))
        blocks.append(jnp.where(seq == 0, both[0], both[1]))
    for j, out in enumerate(outs):
        out[...] = choose(lax.bitwise_xor(lo, j), blocks).astype(BF16)


def order_columns_kernel(joint, own, a, b, c, down_ref, proj_ref, qkv_ref, rest_ref):
    lo = lo_index()
    got = [ref[...].astype(F32) for ref in (own, a, b, c)]
    deep = got[0].shape[0]
    blocks = [choose(lax.bitwise_xor(lo, j), got) for j in range(4)]
    third = proj_ref.shape[1] // 3
    for j in range(4):
        qkv_ref[j, :, :joint] = blocks[j][:, :joint].astype(BF16)
        if j < 3:
            qkv_ref[j, :, joint:] = proj_ref[:, j * third : (j + 1) * third]
        else:
            qkv_ref[j, :, joint:] = jnp.zeros((deep, third), BF16)
    down = down_ref[...].astype(F32)
    down = jnp.where(lax.axis_index("seq") == 0, down[: 2 * deep], down[2 * deep :])
    for i in range(2):
        up = jnp.concatenate((blocks[i][:, joint:], blocks[2 + i][:, joint:]), axis=1)
        rest_ref[i] = up.astype(BF16)
        rest_ref[2 + i] = down[i * deep : (i + 1) * deep].astype(BF16)


def split_first_kernel(got_ref, qkv_ref, proj_ref):
    joint = qkv_ref.shape[2]
    third = got_ref.shape[2] - joint
    for g in range(got_ref.shape[0]):
        qkv_ref[g] = got_ref[g, :, :joint]
        if g % 4 < 3:
            proj_ref[g // 4, :, (g % 4) * third : (g % 4 + 1) * third] = got_ref[g, :, joint:]


def split_kernel(far, got_ref, up_ref, down_ref):
    for z in range(far):
        for i in range(2):
            pair = got_ref[4 * z + i].astype(F32)
            n = pair.shape[1] // 2
            up_ref[4 * z + i] = pair[:, :n].astype(BF16)
            up_ref[4 * z + 2 + i] = pair[:, n:].astype(BF16)
            down_ref[2 * z + i] = got_ref[4 * z + 2 + i]


def order_skip_kernel(deep, lo_f, *refs):
    *blocks, w_ref, vec_ref, up_ref = refs
    n = len(blocks)
    k = w_ref.shape[1]
    far, lo, seq = lax.axis_index("far"), lo_index(), lax.axis_index("seq")
    got = [ref[...].astype(F32) for ref in blocks]
    for j, v in enumerate(got):
        w_ref[lax.rem(far - j + n, n)] = v[:k].astype(BF16)
    lines = [choose(lax.rem(far - z + n, n), [v[k : k + 1] for v in got]) for z in range(n)]
    up_ref[...] = jnp.concatenate(
        [jnp.where(seq == 0, v[:, :lo_f], v[:, lo_f : 2 * lo_f]) for v in lines], axis=1
    )
    pieces = []
    for v in lines:
        tall = [v[:, 2 * lo_f + i * deep : 2 * lo_f + (i + 1) * deep] for i in range(7)]
        tall = jnp.concatenate([jnp.zeros_like(tall[0])] + tall, axis=0)
        pieces += [jnp.where((lo == j) & (seq == 0), tall, 0.0) for j in range(4)]
    vec_ref[...] = jnp.concatenate(pieces, axis=1)


def unpack_kernel(half, quarter, k, got_ref, x_ref, s_ref, wide):
    part = x_ref.shape[0]
    got = [got_ref[r, 0:part, :].astype(F32) for r in range(8)]
    x_ref[...] = jnp.concatenate(
        [got[r][:, j * k : (j + 1) * k] for j in range(half) for r in range(8)], axis=1
    ).astype(BF16)
    for t in range(2):
        base = half + t * quarter
        wide[t * part : (t + 1) * part, :] = jnp.concatenate(
            [got[r][:, (base + j) * k : (base + j + 1) * k] for j in range(quarter) for r in range(8)],
            axis=1,
        )
    s_ref[...] = wide[...].astype(BF16)


def unpack_call(run, got, part, half, quarter, k):
    width = 8 * half * k
    return run(
        functools.partial(unpack_kernel, half, quarter, k),
        (shape((part, width), BF16), shape((2 * part, width // 2), BF16)),
        got,
        scratch=[pltpu.VMEM((2 * part, width // 2), F32)],
        name="unpack",
    )


def halves(h, q, a, b):
    zero = jnp.concatenate((a[:, :h], a[:, h : h + q], b[:, h : h + q]), axis=1)
    one = jnp.concatenate((b[:, :h], a[:, h + q :], b[:, h + q :]), axis=1)
    return zero, one


def skip_kernel(side, part, h, q, got_ref, w_ref, vec_ref, x_ref, out_ref):
    near, core, seq = (lax.axis_index(name) for name in TEAM)
    real = lax.broadcasted_iota(jnp.int32, (got_ref.shape[1], 1), 0) < part
    for fn in range(2):
        base = lax.bitwise_xor(near, fn) * 4 + lax.bitwise_xor(core, side) * 2
        zero, one = halves(h, q, got_ref[base].astype(F32), got_ref[base + 1].astype(F32))
        mine = jnp.where(seq == 0, zero, one)
        other = jnp.where(seq == 0, one, zero)
        for i, x in enumerate((mine, other)):
            x = jnp.where(real, x, 0.0).astype(BF16)
            x_ref[2 * fn + i] = x
            out = nn(x, w_ref[...])
            base = out.shape[0] - 8
            out = jnp.concatenate((out[:base], out[base:] + vec_ref[...]), axis=0)
            out_ref[2 * fn + i] = out.astype(out_ref.dtype)


def skip_call(run, side, part, h, q, got, w, vec, kind):
    _, rows, deep = got.shape
    return run(
        functools.partial(skip_kernel, side, part, h, q),
        (shape((4, rows, deep), BF16), shape((4, rows, w.shape[1]), kind)),
        got,
        w,
        vec,
        name="skip",
    )


def turn_kernel(x0_ref, x1_ref, out_ref):
    for i, ref in enumerate((x0_ref, x1_ref)):
        for j in range(4):
            out_ref[4 * i + j] = ref[j].astype(F32).T.astype(BF16)


def skip_back_kernel(h, q, d0_ref, d1_ref, w_ref, out_ref):
    near, core, seq = (lax.axis_index(name) for name in TEAM)
    for side, d_ref in enumerate((d0_ref, d1_ref)):
        for fn in range(2):
            base = lax.bitwise_xor(near, fn) * 4 + lax.bitwise_xor(core, side) * 2
            mine = nt(d_ref[2 * fn], w_ref[...])
            other = nt(d_ref[2 * fn + 1], w_ref[...])
            zero = jnp.where(seq == 0, mine, other)
            one = jnp.where(seq == 0, other, mine)
            out_ref[base] = jnp.concatenate(
                (zero[:, :h], zero[:, h : h + q], one[:, h : h + q]), axis=1
            ).astype(BF16)
            out_ref[base + 1] = jnp.concatenate(
                (one[:, :h], zero[:, h + q :], one[:, h + q :]), axis=1
            ).astype(BF16)


def skip_back_call(run, h, q, dh, w):
    rows = dh[0].shape[1]
    return run(
        functools.partial(skip_back_kernel, h, q),
        shape((8, rows, w.shape[0]), BF16),
        dh[0],
        dh[1],
        w,
        name="skip_back",
    )


def merge_kernel(mine_ref, got_ref, *outs):
    for i, out in enumerate(outs):
        out[...] = (mine_ref[i + 1] + got_ref[i + 1].astype(F32)).astype(BF16)


def stack_kernel(a, b, c, d, out_ref):
    for i, ref in enumerate((a, b, c, d)):
        out_ref[i] = ref[...]


def arrived(mine_ref, got_ref, others):
    total = mine_ref[0] + got_ref[0].astype(F32)
    for ref in others:
        total = total + ref[...].astype(F32)
    return total


def normalized(total, gain, shift):
    center = total - jnp.mean(total, axis=-1, keepdims=True)
    spread = jnp.mean(center * center, axis=-1, keepdims=True)
    return (center * lax.rsqrt(spread + EPS) * gain + shift).astype(BF16)


def norm_first_kernel(mine, got, b, c, d, total_ref, normed_ref, vec_ref):
    total = arrived(mine, got, (b, c, d))
    vec_ref[...] = total[total.shape[0] - 8 :]
    bias, gain, shift = (vec_ref[i : i + 1, :] for i in (1, 2, 3))
    total = total + bias
    total_ref[...] = total
    normed_ref[...] = normalized(total, gain, shift)


def norm_second_kernel(base, mine, got, b, c, d, vec_ref, total_ref, normed_ref):
    bias, gain, shift = (vec_ref[i : i + 1, :] for i in (4, 5, 6))
    total = arrived(mine, got, (b, c, d)) + bias + base[...]
    total_ref[...] = total
    normed_ref[...] = normalized(total, gain, shift)


def norm_back_kernel(place, part, mine, got, b, c, d, total_ref, vec_ref, resid, wide_ref, low_ref):
    grad = arrived(mine, got, (b, c, d))
    gain = vec_ref[place : place + 1, :]
    center = total_ref[...] - jnp.mean(total_ref[...], axis=-1, keepdims=True)
    spread = jnp.mean(center * center, axis=-1, keepdims=True)
    scale = lax.rsqrt(spread + EPS)
    unit = center * scale
    inner = grad * gain
    back = inner - jnp.mean(inner, axis=-1, keepdims=True)
    back = (back - unit * jnp.mean(inner * unit, axis=-1, keepdims=True)) * scale
    wide = resid[...] + back
    if wide_ref is not None:
        wide_ref[...] = wide
    d_gain = jnp.sum(grad * unit, axis=0, keepdims=True)
    d_shift = jnp.sum(grad, axis=0, keepdims=True)
    row = lax.broadcasted_iota(jnp.int32, (wide.shape[0], 1), 0)
    wide = jnp.where(row < part, wide, 0.0)
    for i, v in enumerate((d_gain, d_shift)):
        high = v.astype(BF16).astype(F32)
        wide = jnp.where(row == part + 2 * i, high, wide)
        wide = jnp.where(row == part + 2 * i + 1, v - high, wide)
    low_ref[...] = wide.astype(BF16)


def norm_back_last(place, part, mine, got, b, c, d, total, vec, resid, low_ref):
    norm_back_kernel(place, part, mine, got, b, c, d, total, vec, resid, None, low_ref)


def norm_back_call(run, place, part, parts, total, vec, resid, both):
    low = shape(total.shape, BF16)
    body = functools.partial(norm_back_kernel if both else norm_back_last, place, part)
    outs = (shape(total.shape, F32), low) if both else low
    return run(body, outs, *parts, total, vec, resid, name="norm_back")


def cot_kernel(cot_ref, bins_ref, weights_ref, wide_ref, low_ref):
    part = cot_ref.shape[0]
    wide_ref[...] = jnp.zeros_like(wide_ref)
    wide_ref[0:part, :] = cot_ref[...].astype(F32) * weights_ref[bins_ref[0]]
    low_ref[...] = wide_ref[...].astype(BF16)


def token_place(rows):
    place = lax.broadcasted_iota(jnp.int32, (2 * rows, 1), 0)
    return jnp.where(place >= rows, place - rows, place)


def head_masks(width):
    lane = lax.broadcasted_iota(jnp.int32, (1, width), 1)
    return [
        jnp.where((lane >= i * HEAD_DIM) & (lane < (i + 1) * HEAD_DIM), 1.0, 0.0).astype(BF16)
        for i in range(width // HEAD_DIM)
    ]


def probs_of(k, q, bias):
    scores = nt(k, q) * (HEAD_DIM**-0.5) + bias
    expo = jnp.exp(scores - jnp.max(scores, axis=0, keepdims=True))
    return expo * (1.0 / jnp.sum(expo, axis=0, keepdims=True))


def split3(v, width):
    return (v[:, i * width : (i + 1) * width] for i in range(3))


def attend_kernel(part, x_ref, qkv_ref, proj_ref, joined_ref, mixed_ref, out_ref):
    rows = out_ref.shape[1]
    seq = lax.axis_index("seq") if proj_ref.shape[0] > 1 else 0
    real = token_place(rows) < part
    bias = jnp.where(real, 0.0, -1e30).astype(F32)
    for item in range(x_ref.shape[0]):
        joined = nn(x_ref[item], qkv_ref[...]).astype(BF16)
        joined_ref[item] = joined
        q, k, v = split3(joined, mixed_ref.shape[2])
        mixed = None
        for mask in head_masks(q.shape[1]):
            probs = probs_of(k, q * mask, bias).astype(BF16)
            term = tn(probs, v * mask)
            mixed = term if mixed is None else mixed + term
        mixed = jnp.where(real, mixed, 0.0).astype(BF16)
        mixed_ref[item] = mixed
        out = nn(mixed, proj_ref[seq])
        out_ref[2 * item] = out[:rows].astype(out_ref.dtype)
        out_ref[2 * item + 1] = out[rows:].astype(out_ref.dtype)


def attend_call(run, part, x, w_qkv, w_proj, kind):
    items, rows, width = x.shape
    inner = w_proj.shape[1]
    return run(
        functools.partial(attend_kernel, part),
        (
            shape((items, rows, w_qkv.shape[1]), BF16),
            shape((items, rows, inner), BF16),
            shape((2 * items, rows // 2, width), kind),
        ),
        x,
        w_qkv,
        w_proj,
        name="attend",
        cost=LITTLE,
    )


def attend_back_kernel(part, d_ref, joined_ref, qkv_ref, proj_ref, grads_ref, out_ref):
    rows = out_ref.shape[1]
    real = token_place(rows) < part
    bias = jnp.where(real, 0.0, -1e30).astype(F32)
    factor = HEAD_DIM**-0.5
    seq = lax.axis_index("seq") if proj_ref.shape[0] > 1 else 0
    for item in range(d_ref.shape[0]):
        d_mixed = nt(d_ref[item], proj_ref[seq])
        d_mixed = jnp.where(real, d_mixed, 0.0).astype(BF16)
        q, k, v = split3(joined_ref[item], proj_ref.shape[1])
        d_q = d_k = d_v = 0.0
        for mask in head_masks(q.shape[1]):
            probs = probs_of(k, q * mask, bias)
            d_one = d_mixed * mask
            d_v = d_v + nn(probs.astype(BF16), d_one)
            d_probs = nt(v, d_one)
            inner = jnp.sum(d_probs * probs, axis=0, keepdims=True)
            d_scores = (probs * (d_probs - inner)).astype(BF16)
            d_k = d_k + nn(d_scores, q * mask)
            d_q = d_q + tn(d_scores, k * mask)
        spare = jnp.zeros((2 * rows, grads_ref.shape[2] - 3 * d_v.shape[1]), F32)
        grads = jnp.concatenate((d_q * factor, d_k * factor, d_v, spare), axis=1).astype(BF16)
        grads_ref[item] = grads
        out = nt(grads, qkv_ref[...])
        out_ref[2 * item] = out[:rows].astype(out_ref.dtype)
        out_ref[2 * item + 1] = out[rows:].astype(out_ref.dtype)


def attend_back_call(run, part, d, joined, w_qkv, w_proj, kind):
    items, rows, width = d.shape
    return run(
        functools.partial(attend_back_kernel, part),
        (shape(joined.shape, BF16), shape((2 * items, rows // 2, width), kind)),
        d,
        joined,
        w_qkv,
        w_proj,
        name="attend_back",
        cost=3,
    )


def mlp_kernel(x_ref, d_ref, up_ref, bias_ref, down_ref, act_ref, grad_ref, sum_ref, out_ref):
    rows = out_ref.shape[1]
    total = 0.0
    for item in range(x_ref.shape[0]):
        upper = nn(x_ref[item], up_ref[...]) + bias_ref[...]
        bell = 0.5 * (1.0 + lax.erf(upper * (0.5**0.5)))
        act_ref[item] = (upper * bell).astype(BF16)
        slope = bell + upper * jnp.exp(-0.5 * upper * upper) * 0.3989422804014327
        d_upper = (slope * nt(d_ref[item], down_ref[...])).astype(BF16)
        grad_ref[item] = d_upper
        total = total + jnp.sum(d_upper.astype(F32), axis=0, keepdims=True)
        out = nt(d_upper, up_ref[...])
        out_ref[2 * item] = out[:rows].astype(out_ref.dtype)
        out_ref[2 * item + 1] = out[rows:].astype(out_ref.dtype)
    sum_ref[...] = total


def mlp_call(run, x, d, w_up, b_up, w_down, kind):
    items, rows, width = x.shape
    inner = w_up.shape[1]
    return run(
        mlp_kernel,
        (
            shape((items, rows, inner), BF16),
            shape((items, rows, inner), BF16),
            shape((1, inner), F32),
            shape((2 * items, rows // 2, width), kind),
        ),
        x,
        d,
        w_up,
        b_up,
        w_down,
        name="mlp",
    )


def down_kernel(act_ref, w_ref, out_ref):
    rows = out_ref.shape[1]
    for item in range(act_ref.shape[0]):
        out = nn(act_ref[item], w_ref[...])
        out_ref[2 * item] = out[:rows].astype(out_ref.dtype)
        out_ref[2 * item + 1] = out[rows:].astype(out_ref.dtype)


def down_call(run, act, w, kind):
    items, rows, _ = act.shape
    dims = (2 * items, rows // 2, w.shape[1])
    return run(down_kernel, shape(dims, kind), act, w, name="down", cost=WINDOW)


def output_kernel(place, base, mine, got, b, c, d, vec_ref, out_ref):
    total = base[...] + arrived(mine, got, (b, c, d)) + vec_ref[place : place + 1, :]
    out_ref[...] = total[: out_ref.shape[0]].astype(BF16)


def product_kernel(*refs):
    *sides, out_ref = refs
    total = 0.0
    n = len(sides) // 2
    for left, right in zip(sides[:n], sides[n:]):
        for item in range(left.shape[0]):
            total = total + tn(left[item], right[item])
    out_ref[...] = total.astype(BF16)


def product_call(run, left, right, name):
    dims = (left[0].shape[-1], right[0].shape[-1])
    return run(product_kernel, shape(dims, BF16), *left, *right, name=name)


def product_two_kernel(far, n20, n21, du0, du1, act0, act1, dm0, dm1, out_ref):
    def product(pairs):
        total = 0.0
        for left, right in pairs:
            for item in range(2):
                total = total + tn(left[item], right[item])
        return total

    deep = out_ref.shape[2]
    down = product(((act0, dm0), (act1, dm1)))
    for z in range(far):
        for i in range(2):
            at = (2 * z + i) * deep
            out_ref[z, 2 + i] = down[at : at + deep].astype(BF16)
    up = product(((n20, du0), (n21, du1)))
    for z in range(far):
        for i in range(2):
            at = (4 * z + i) * deep
            pair = (up[at : at + deep], up[at + 2 * deep : at + 3 * deep])
            out_ref[z, i] = jnp.concatenate(pair, axis=1).astype(BF16)


def product_attend_kernel(far, n10, n11, dj0, dj1, a0, a1, d0, d1, out_ref):
    def product(pairs):
        total = 0.0
        for left, right in pairs:
            for item in range(2):
                total = total + tn(left[item], right[item])
        return total

    deep, joint = out_ref.shape[2], dj0.shape[2]
    third = out_ref.shape[3] - joint
    qkv = product(((n10, dj0), (n11, dj1)))
    for z in range(far):
        for j in range(4):
            at = (4 * z + j) * deep
            out_ref[z, j, :, :joint] = qkv[at : at + deep].astype(BF16)
    proj = product(((a0, d0), (a1, d1)))
    seq = lax.axis_index("seq")
    for z in range(far):
        at = z % 2 * deep
        rows = jnp.where(seq == z // 2, proj[at : at + deep], 0.0).astype(BF16)
        for j in range(4):
            cut = rows[:, j * third : (j + 1) * third] if j < 3 else jnp.zeros((deep, third), BF16)
            out_ref[z, j, :, joint:] = cut


def double_up_kernel(got_ref, up_ref, down_ref):
    n = up_ref.shape[2]
    for j in range(4):
        v = got_ref[j % 2].astype(F32)[:, (j // 2) * n : (j // 2 + 1) * n].astype(BF16)
        up_ref[2 * j] = v
        up_ref[2 * j + 1] = v
    for i in range(2):
        down_ref[i] = got_ref[2 + i]


def double_qkv_kernel(got_ref, qkv_ref, proj_ref):
    joint = qkv_ref.shape[2]
    third = got_ref.shape[2] - joint
    for j in range(4):
        v = got_ref[j, :, :joint]
        qkv_ref[2 * j] = v
        qkv_ref[2 * j + 1] = v
        if j < 3:
            proj_ref[:, j * third : (j + 1) * third] = got_ref[j, :, joint:]


def pair_sum_kernel(a_ref, b_ref, out_ref):
    out_ref[...] = a_ref[...].astype(F32) + b_ref[...].astype(F32)


def sums_kernel(part, rows, da0, da1, dm0, dm1, out_ref):
    lines = block_sums(part, rows, (da0, da1), True) + block_sums(part, rows, (dm0, dm1), False)
    out_ref[...] = jnp.concatenate(lines + [jnp.zeros((4, da0.shape[-1]), F32)], axis=0)


def block_sums(part, rows, refs, extra):
    place = token_place(rows)
    sums = [0.0, 0.0, 0.0]
    for ref in refs:
        for item in range(2):
            v = ref[item].astype(F32)
            sums[0] = sums[0] + jnp.sum(jnp.where(place < part, v, 0.0), axis=0, keepdims=True)
            if extra:
                for i in range(2):
                    at = (place == part + 2 * i) | (place == part + 2 * i + 1)
                    sums[1 + i] = sums[1 + i] + jnp.sum(jnp.where(at, v, 0.0), axis=0, keepdims=True)
    return sums if extra else sums[:1]


def vector_kernel(far, deep, part, rows, xt_ref, dh0, dh1, sums_ref, s0, s1, out_ref):
    lo = lax.axis_index("near") * 2 + lax.axis_index("core")
    width = dh0.shape[-1]
    total = 0.0
    for side, ref in enumerate((dh0, dh1)):
        for item in range(2):
            d = ref[item]
            for i in range(2):
                total = total + nn(xt_ref[4 * side + 2 * item + i], d[i * rows : (i + 1) * rows])
    k = total.shape[0] // far
    lines = block_sums(part, rows, (dh0, dh1), True)
    stacked = jnp.concatenate(lines + [sums_ref[i : i + 1, :] for i in range(5)], axis=0)
    up = s0[...] + s1[...]
    f = up.shape[1] // far
    spare = jnp.zeros((8, width - 2 * f), F32)
    row = lax.broadcasted_iota(jnp.int32, (8, 1), 0)
    for z in range(far):
        cut = 0.0
        for j in range(4):
            at = (z * 4 + j) * deep
            cut = cut + jnp.where(lo == j, stacked[:, at : at + deep], 0.0)
        low = jnp.concatenate((cut, jnp.zeros((8, 2 * f - deep), F32)), axis=1)
        tall = jnp.concatenate((up[:, z * f : (z + 1) * f], jnp.zeros((1, f), F32)), axis=1)
        low = jnp.where(row == 7, tall, low)
        low = jnp.concatenate((low, spare), axis=1)
        out_ref[z] = jnp.concatenate((total[z * k : (z + 1) * k], low), axis=0).astype(BF16)


def two_halves_kernel(mine_ref, other_ref, out_ref):
    seq = lax.axis_index("seq")
    k = mine_ref.shape[1]
    for i in range(2):
        mine, other = mine_ref[i].astype(F32), other_ref[i].astype(F32)
        out_ref[i * k : (i + 1) * k, :] = jnp.where(seq == 0, mine, other)
        out_ref[(2 + i) * k : (3 + i) * k, :] = jnp.where(seq == 0, other, mine)


def last_kernel(k, deep, f, mine_ref, other_ref, out_ref, vec_ref, up_ref):
    seq = lax.axis_index("seq")
    mine, other = mine_ref[...].astype(F32), other_ref[...].astype(F32)
    zero = jnp.where(seq == 0, mine, other)
    one = jnp.where(seq == 0, other, mine)
    out_ref[0:k, :] = zero[:k]
    out_ref[k : 2 * k, :] = one[:k]
    vec_ref[...] = mine[k : k + 8, :deep]
    up_ref[...] = jnp.concatenate((zero[k + 7 : k + 8, :f], one[k + 7 : k + 8, :f]), axis=1)


def columns_kernel(order, got_ref, out_ref):
    got = [got_ref[i].astype(F32) for i in range(8)]
    out_ref[...] = jnp.concatenate([got[2 * lo + s][:, at : at + n] for s, lo, at, n in order], axis=1)


def columns_call(run, order, got, name):
    wide = sum(n for *_, n in order)
    return run(functools.partial(columns_kernel, order), shape((got.shape[1], wide), F32), got, name=name)


def swap(v, *axes):
    return lax.ppermute(v, axes if len(axes) > 1 else axes[0], FLIP4 if len(axes) > 1 else FLIP2)


def send_own(own):
    return own, swap(own, "seq"), swap(own, "near"), swap(own, "near", "seq")


def spread_blocks(run, parts):
    rows, width = parts[0].shape
    quad = run(stack_kernel, shape((4, rows, width), BF16), *parts, name="stack")
    other = swap(quad, "core")
    return quad.reshape(2, 2 * rows, width), other.reshape(2, 2 * rows, width)


def collect_blocks(run, mine, got):
    one = shape(mine.shape[1:], BF16)
    b, c, d = run(merge_kernel, (one, one, one), mine, got, name="merge")
    return mine, got, swap(b, "seq"), swap(c, "near"), swap(d, "near", "seq")


def from_far(v, far):
    return [v] + [lax.ppermute(v, "far", [(i, (i + j) % far) for i in range(far)]) for j in range(1, far)]


def to_far(blocks, far):
    return [blocks[0]] + [
        lax.ppermute(blocks[j], "far", [(i, (i + j) % far) for i in range(far)]) for j in range(1, far)
    ]


def gather_far(v):
    return lax.all_gather(v, "far", axis=0, tiled=False)


def pick(v, at, axis):
    return lax.dynamic_index_in_dim(v, at, axis, keepdims=False)


def body(
    inputs,
    skips,
    cotangent,
    bins,
    bin_weights,
    skip_w,
    skip_b,
    ln1_g,
    ln1_b,
    qkv_w,
    proj_w,
    proj_b,
    ln2_g,
    ln2_b,
    fc1_w,
    fc1_b,
    fc2_w,
    fc2_b,
    *,
    far,
):
    _, part, width = inputs.shape
    rows = -(-part // 8) * 8
    dp = far * 4
    seq = lax.axis_index("seq")
    lo = lax.axis_index("near") * 2 + lax.axis_index("core")
    per = HEADS // 8
    inner = per * HEAD_DIM
    joint = -(-3 * inner // 128) * 128
    deep = width // dp
    k = skip_w.shape[0] // 2
    f = fc2_w.shape[0] // 2
    half, quarter = far // 2, far // 4
    spread = far * k
    one_head = dp == HEADS

    run = Line()

    sent = pack_call(run, inputs[0], skips[0], rows, half, quarter, k)
    got = lax.all_to_all(sent, TEAM, split_axis=0, concat_axis=0, tiled=True)
    small = tuple(v.reshape(1, -1) for v in (fc1_b, skip_b, ln1_g, ln1_b, proj_b, ln2_g, ln2_b, fc2_b))
    skip_half = run(
        skip_half_kernel, shape((k + 8, width), BF16), skip_w, *small, name="skip_half", cost=FIRST
    )
    skip_blocks = from_far(skip_half, far)
    columns = run(
        functools.partial(pack_columns_kernel, far, per, joint, f),
        (shape((deep, joint + far * f), BF16),) * 4,
        qkv_w,
        fc1_w,
        name="pack_columns",
        cost=FIRST,
    )
    columns = (columns[0], swap(columns[1], "core"), swap(columns[2], "near"), swap(columns[3], "near", "core"))
    w_skip, vec, b_up = run(
        functools.partial(order_skip_kernel, deep, f),
        (shape((far, k, width), BF16), shape((8, width), F32), shape((1, far * f), F32)),
        *skip_blocks,
        name="order_skip",
    )
    w_skip = w_skip.reshape(spread, width)
    qkv_part, rest = run(
        functools.partial(order_columns_kernel, joint),
        (shape((4, deep, joint + width // 3), BF16), shape((4, deep, width), BF16)),
        *columns,
        fc2_w,
        proj_w,
        name="order_columns",
    )
    first = gather_far(qkv_part).reshape(dp, deep, joint + width // 3)
    rest = gather_far(rest).reshape(4 * far, deep, width)
    x1, theirs = skip_call(run, 1, part, half * k, quarter * k, got, w_skip, vec, BF16)
    pair = swap(theirs, "core")
    x0, mine = skip_call(run, 0, part, half * k, quarter * k, got, w_skip, vec, F32)
    come = collect_blocks(run, mine, pair)
    x_turned = run(turn_kernel, shape((8, spread, rows), BF16), x0, x1, name="turn")
    d_wide, d_own = run(
        cot_kernel,
        (shape((rows, width), F32), shape((rows, width), BF16)),
        cotangent[0],
        name="cot",
        scalars=(bins, bin_weights),
    )
    hidden, normed, vec = run(
        norm_first_kernel,
        (shape((rows, width), F32), shape((rows, width), BF16), shape((8, width), F32)),
        *come,
        name="norm",
    )

    parts = send_own(normed)
    n1 = spread_blocks(run, parts)
    w_qkv, w_proj = run(
        split_first_kernel,
        (shape((dp, deep, joint), BF16), shape((far, deep, width), BF16)),
        first,
        name="split_first",
    )
    w_qkv = w_qkv.reshape(width, joint)
    if one_head:
        w_proj = w_proj.reshape(2, inner, width)
    else:
        w_proj = lax.all_gather(proj_w, ("far", "near", "core"), axis=0, tiled=True)
        w_proj = pick(w_proj.reshape(2, per, 4, HEAD_DIM, width), seq, 0)
        w_proj = pick(w_proj, lo, 1).reshape(1, inner, width)
    joined1, mixed1, theirs = attend_call(run, part, n1[1], w_qkv, w_proj, BF16)
    pair = swap(theirs, "core")
    d_parts = send_own(d_own)
    joined0, mixed0, mine = attend_call(run, part, n1[0], w_qkv, w_proj, F32)
    come = collect_blocks(run, mine, pair)
    d_mlp = spread_blocks(run, d_parts)
    middle, second = run(
        norm_second_kernel,
        (shape((rows, width), F32), shape((rows, width), BF16)),
        hidden,
        *come,
        vec,
        name="norm",
    )

    parts = send_own(second)
    n2 = spread_blocks(run, parts)
    w_up, w_down = run(
        functools.partial(split_kernel, far),
        (shape((4 * far, deep, far * f), BF16), shape((2 * far, deep, width), BF16)),
        rest,
        name="split",
    )
    w_up, w_down = w_up.reshape(width, far * f), w_down.reshape(far * f, width)
    act1, du1, s1, theirs = mlp_call(run, n2[1], d_mlp[1], w_up, b_up, w_down, BF16)
    pair = swap(theirs, "core")
    act0, du0, s0, mine = mlp_call(run, n2[0], d_mlp[0], w_up, b_up, w_down, F32)
    come = collect_blocks(run, mine, pair)

    def scatter(v):
        return lax.psum_scatter(v, "far", scatter_dimension=0, tiled=True)

    def to_team(v):
        return lax.all_to_all(v, TEAM, split_axis=0, concat_axis=0, tiled=True)

    g_rest = run(
        functools.partial(product_two_kernel, far),
        shape((far, 4, deep, width), BF16),
        *n2,
        du0,
        du1,
        act0,
        act1,
        *d_mlp,
        name="grad_mlp",
        cost=WINDOW,
    )
    g_rest = scatter(g_rest.reshape(4 * far, deep, width))
    d_middle, d_branch = norm_back_call(run, 5, part, come, middle, vec, d_wide, True)

    parts = send_own(d_branch)
    out_pair = swap(down_call(run, act1, w_down, BF16), "core")
    out_mine = down_call(run, act0, w_down, F32)
    da = spread_blocks(run, parts)
    out_come = collect_blocks(run, out_mine, out_pair)
    dj1, theirs = attend_back_call(run, part, da[1], joined1, w_qkv, w_proj, BF16)
    pair = swap(theirs, "core")
    dj0, mine = attend_back_call(run, part, da[0], joined0, w_qkv, w_proj, F32)
    output = run(
        functools.partial(output_kernel, 7), shape((part, width), BF16), middle, *out_come, vec, name="output"
    )
    come = collect_blocks(run, mine, pair)
    if one_head:
        g_first = run(
            functools.partial(product_attend_kernel, far),
            shape((far, 4, deep, joint + width // 3), BF16),
            *n1,
            dj0,
            dj1,
            mixed0,
            mixed1,
            *da,
            name="grad_attend",
            cost=WINDOW,
        )
        g_first = scatter(g_first.reshape(4 * far, deep, -1))
    else:
        g_qkv = scatter(product_call(run, n1, (dj0, dj1), "grad_qkv")).reshape(4, deep, joint)
        g_first = jnp.pad(g_qkv, ((0, 0), (0, 0), (0, width // 3)))
        g_proj = product_call(run, (mixed0, mixed1), da, "grad_proj")
        spot = jnp.zeros((2, per, 4, HEAD_DIM, width), BF16)
        spot = lax.dynamic_update_slice(
            spot, g_proj.reshape(1, per, 1, HEAD_DIM, width), (seq, 0, lo, 0, 0)
        )
        low_own = lax.psum_scatter(
            spot.reshape(width, width), ("far", "near", "core"), scatter_dimension=0, tiled=True
        )
    g_up, g_down = run(
        double_up_kernel,
        (shape((8, deep, far * f), BF16), shape((2, deep, width), BF16)),
        g_rest,
        name="double_up",
        cost=WINDOW,
    )
    g_up = to_team(g_up)
    down_other = swap(g_down, "seq")
    d_hidden = norm_back_call(run, 2, part, come, hidden, vec, d_middle, False)

    parts = send_own(d_hidden)
    early = run(
        functools.partial(sums_kernel, part, rows), shape((8, width), F32), *da, *d_mlp, name="sums", cost=WINDOW
    )
    dh = spread_blocks(run, parts)
    g_skip = run(
        functools.partial(vector_kernel, far, deep, part, rows),
        shape((far, k + 8, width), BF16),
        x_turned,
        *dh,
        early,
        s0,
        s1,
        name="grad_skip",
    )
    g_skip = scatter(g_skip.reshape(far * (k + 8), width))
    blocks = tuple(v.reshape(4, rows, width) for v in dh)
    sent = skip_back_call(run, half * k, quarter * k, blocks, w_skip)
    got = lax.all_to_all(sent, TEAM, split_axis=0, concat_axis=0, tiled=True)
    order = [(s, j, z * f, f) for z in range(far) for j in range(4) for s in range(2)]
    d_fc1_w = columns_call(run, order, g_up, "whole_up")
    d_fc2_w = run(two_halves_kernel, shape((2 * f, width), F32), g_down, down_other, name="whole_down")
    g_qkv, low = run(
        double_qkv_kernel,
        (shape((8, deep, joint), BF16), shape((deep, width), BF16)),
        g_first,
        name="double_qkv",
    )
    g_qkv = to_team(g_qkv)
    if not one_head:
        low = low_own
    low_other = swap(low, "seq")

    d_inputs, d_skips = unpack_call(run, got, part, half, quarter, k)
    order = [
        (s, j, (b * per + i) * HEAD_DIM, HEAD_DIM)
        for b in range(3)
        for s in range(2)
        for i in range(per)
        for j in range(4)
    ]
    d_qkv_w = columns_call(run, order, g_qkv, "whole_qkv")
    d_proj_w = run(pair_sum_kernel, shape(low.shape, F32), low, low_other, name="whole_proj")
    d_skip_w, vectors, d_up_b = run(
        functools.partial(last_kernel, k, deep, f),
        (shape((2 * k, width), F32), shape((8, deep), F32), shape((1, 2 * f), F32)),
        g_skip,
        swap(g_skip, "seq"),
        name="whole_skip",
    )
    return (
        output.reshape(1, part, width),
        d_inputs.reshape(1, part, width),
        d_skips.reshape(1, 2 * part, width // 2),
        d_skip_w,
        vectors[0],
        vectors[1],
        vectors[2],
        d_qkv_w,
        d_proj_w,
        vectors[3],
        vectors[4],
        vectors[5],
        d_fc1_w,
        d_up_b.reshape(2 * f),
        d_fc2_w,
        vectors[6],
    )


def solution(mesh):
    dp, seq = mesh.shape["dp"], mesh.shape["seq"]
    far = dp // 4
    fine = Mesh(mesh.devices.reshape(far, 2, 2, seq), ("far", "near", "core", "seq"))
    items = ("far", "near", "core")
    tokens = P(items, "seq", None)
    features = P(items, None, "seq")
    matrix = P(items, None)
    vector = P(items)
    in_specs = (
        tokens,
        features,
        tokens,
        vector,
        P(),
        matrix,
        vector,
        vector,
        vector,
        matrix,
        matrix,
        vector,
        vector,
        vector,
        matrix,
        vector,
        matrix,
        vector,
    )
    out_specs = (
        tokens,
        tokens,
        features,
        matrix,
        vector,
        vector,
        vector,
        matrix,
        matrix,
        vector,
        vector,
        vector,
        matrix,
        vector,
        matrix,
        vector,
    )
    return jax.shard_map(
        functools.partial(body, far=far),
        mesh=fine,
        in_specs=in_specs,
        out_specs=out_specs,
        check_vma=False,
    )
```

time: 563 us -> 346 us (0.61)
  blocking collectives: 195 us -> 0 us
  waiting for transfers between devices: 98.3 us -> 152 us
  local copies, waits for them, and re-layouts: 75.9 us -> 23.8 us
  matrix products: 38.8 us -> 0 us
  Pallas kernels: 55 us -> 88.4 us
  other arithmetic: 23 us -> 0.6 us
  starting transfers between devices: 55.2 us -> 65.6 us
    all_gather x6 -> x0, blocking collectives: 76.7 us -> none  [the longest x2 39.9 us: gather_far(): return lax.all_gather(v, 'far', axis=0, tiled=False)]
    unnamed x1 -> x0, blocking collectives: 60.8 us -> none
    psum x1 -> x0, blocking collectives: 44.4 us -> none  [body(): here = lax.psum(here, ('far', 'near', 'core', 'seq'))]
    dot_general x14 -> x0, matrix products: 38.8 us -> none  [the longest x10 30.7 us: tn(): lax.dot_general(a, b, (((0,), (0,)), ((), ())), preferred_element_type=F32)]
    pallas_call x10 -> x47, Pallas kernels: 55 us -> 88.4 us  [__call__(): pl.pallas_call(call, out_shape=outs + (jax.ShapeDtypeStruct((8, 128), F32...]
    ppermute x41 -> x46, waiting for transfers between devices: 98.1 us -> 128 us  [swap(): lax.ppermute(v, axes if len(axes) > 1 else axes[0], FLIP4 if len(axes) >...]
    convert_element_type x9 -> x0, local copies, waits for them, and re-layouts: 18.9 us -> none  [the longest x3 11 us: body(): d_fc1_w = d_fc1_w.reshape(deep, hidden_all).astype(F32)]
    unnamed x133 -> x140, local copies, waits for them, and re-layouts: 5.83 us -> 22.6 us
  transfers between devices with their start and end apart: 52 -> 58, of which waited for: 24 -> 32; matrix products, arithmetic and copies ran while one was open for 21% -> 0% of each run, Pallas kernels for 7% -> 23%
where the time goes in v2:
time: 346 us
  waiting for transfers between devices  152 us (44%)
  Pallas kernels  88.4 us (26%)
  starting transfers between devices  65.6 us (19%)
  local copies, waits for them, and re-layouts  23.8 us (7%)
  between operations  15.5 us (4%)
    ppermute x46, waiting for transfers between devices, swap(): lax.ppermute(v, axes if len(axes) > 1 else axes[0], FLIP4 if len(axes) >...  128 us
    pallas_call x47, Pallas kernels, __call__(): pl.pallas_call(call, out_shape=outs + (jax.ShapeDtypeStruct((8, 128), F32...  88.4 us
    ppermute x46, starting transfers between devices, swap(): lax.ppermute(v, axes if len(axes) > 1 else axes[0], FLIP4 if len(axes) >...  43.9 us
    unnamed x140, local copies, waits for them, and re-layouts  22.6 us
    all_to_all x2, waiting for transfers between devices, to_team(): return lax.all_to_all(v, TEAM, split_axis=0, concat_axis=0, tiled=True)  10.2 us
    all_to_all x2, starting transfers between devices, to_team(): return lax.all_to_all(v, TEAM, split_axis=0, concat_axis=0, tiled=True)  7.76 us
    ppermute x3, waiting for transfers between devices, from_far(): lax.ppermute(v, 'far', [(i, (i + j) % far) for i in range(far)])  7.69 us
    all_to_all x2, starting transfers between devices, body(): got = lax.all_to_all(sent, TEAM, split_axis=0, concat_axis=0, tiled=True)  7.28 us
  transfers between devices with their start and end apart: 58, of which 32 were waited for; matrix products, arithmetic and copies ran while one was open for 0% of the time, Pallas kernels for 23%

profile of v2, /device:TPU:0, one launch (start us, length us, event | category | flops | bytes accessed | tf_op | source)
XLA Modules:
  0.0 345.8 jit_solution(9121008676522750745)
XLA Ops:
  11.5 5.1 %collective-permute-start.2 = (bf16[80,1152]{1,0:T(8,128)(2,1)S(1)}, bf16[80,1152]{1,0:T(8,128)(2,1)S(1)}, u32[]{:S(2)}, u32[]{:S(2)}) collective-permute-start(bf16[80,1152]{1,0:T(8,128)(2,1)S(1)} %get-tuple-element.153.refs_0_), channel_id=1, source_target_pairs={{0,24},{8,0},{16,8},{24,16},{1,25},{9,1},{17,9},{25,17},{2,26},{10... | collective-permute-start | bytes 552968 | tf_op jit(solution)/shard_map/ppermute | solution.py:725
  24.6 7.7 %collective-permute-done.1.refs_2_ = bf16[80,1152]{1,0:T(8,128)(2,1)S(1)} collective-permute-done((bf16[80,1152]{1,0:T(8,128)(2,1)S(1)}, bf16[80,1152]{1,0:T(8,128)(2,1)S(1)}, u32[]{:S(2)}, u32[]{:S(2)}) %collective-permute-start.1) | collective-permute-done | bytes 184352 | tf_op jit(solution)/shard_map/ppermute | solution.py:725
  32.5 5.1 %collective-permute-done.4.refs_2_ = bf16[72,1088]{1,0:T(8,128)(2,1)S(1)} collective-permute-done((bf16[72,1088]{1,0:T(8,128)(2,1)S(1)}, bf16[72,1088]{1,0:T(8,128)(2,1)S(1)}, u32[]{:S(2)}, u32[]{:S(2)}) %collective-permute-start.4) | collective-permute-done | bytes 156704 | tf_op jit(solution)/shard_map/ppermute | solution.py:704
  57.8 5.8 %collective-permute-done.9.refs_4_ = bf16[136,1152]{1,0:T(8,128)(2,1)S(1)} collective-permute-done((bf16[136,1152]{1,0:T(8,128)(2,1)S(1)}, bf16[136,1152]{1,0:T(8,128)(2,1)S(1)}, u32[]{:S(2)}, u32[]{:S(2)}) %collective-permute-start.9) | collective-permute-done | bytes 313376 | tf_op jit(solution)/shard_map/ppermute | solution.py:704
  67.5 7.8 %collective-permute-done.12.refs_3_ = bf16[136,1152]{1,0:T(8,128)(2,1)S(1)} collective-permute-done((bf16[136,1152]{1,0:T(8,128)(2,1)S(1)}, bf16[136,1152]{1,0:T(8,128)(2,1)S(1)}, u32[]{:S(2)}, u32[]{:S(2)}) %collective-permute-start.12) | collective-permute-done | bytes 313376 | tf_op jit(solution)/shard_map/ppermute | solution.py:704
  75.3 5.0 %collective-permute-done.11.refs_2_ = bf16[136,1152]{1,0:T(8,128)(2,1)S(1)} collective-permute-done((bf16[136,1152]{1,0:T(8,128)(2,1)S(1)}, bf16[136,1152]{1,0:T(8,128)(2,1)S(1)}, u32[]{:S(2)}, u32[]{:S(2)}) %collective-permute-start.11) | collective-permute-done | bytes 313376 | tf_op jit(solution)/shard_map/ppermute | solution.py:704
  81.0 5.6 %all-gather.5.cloned.1.call-done.refs_0_ = bf16[16,72,896]{2,1,0:T(8,128)(2,1)} async-done(((bf16[4,72,896]{2,1,0:T(8,128)(2,1)}), bf16[16,72,896]{2,1,0:T(8,128)(2,1)}) %all-gather.5.cloned.1.call-update) | async-done | bytes 2064400 | tf_op jit(solution)/shard_map/all_gather | solution.py:735
  88.3 5.4 %attend.2 = (bf16[2,272,512]{2,1,0:T(8,128)(2,1)S(1)}, bf16[2,272,144]{2,1,0:T(8,128)(2,1)S(1)}, bf16[4,136,1152]{2,1,0:T(8,128)(2,1)S(1)}, f32[8,128]{1,0:T(8,128)S(1)}) custom-call(bf16[2,272,1152]{2,1,0:T(8,128)(2,1)} %bitcast.14.refs_0_.refs_1_, bf16[1152,512]{1,0:T(8,128)(2,1)S(1)} %bitcast.73, bf16[2,144,1152]{2,1,0:T(8,128)(2,1)S(1)} %bitcast.77, ...), custom_call_target="tpu_custom_call" | custom-call | flops 5000000000 | bytes 1000 | tf_op jit(solution)/shard_map/attend/pallas_call | solution.py:53
  113.2 6.5 %collective-permute-done.15.refs_3_ = bf16[136,1152]{1,0:T(8,128)(2,1)S(1)} collective-permute-done((bf16[136,1152]{1,0:T(8,128)(2,1)S(1)}, bf16[136,1152]{1,0:T(8,128)(2,1)S(1)}, u32[]{:S(2)}, u32[]{:S(2)}) %collective-permute-start.15) | collective-permute-done | bytes 313376 | tf_op jit(solution)/shard_map/ppermute | solution.py:704
  119.8 6.3 %collective-permute-done.17.refs_5_ = bf16[136,1152]{1,0:T(8,128)(2,1)S(1)} collective-permute-done((bf16[136,1152]{1,0:T(8,128)(2,1)S(1)}, bf16[136,1152]{1,0:T(8,128)(2,1)S(1)}, u32[]{:S(2)}, u32[]{:S(2)}) %collective-permute-start.17) | collective-permute-done | bytes 313376 | tf_op jit(solution)/shard_map/ppermute | solution.py:704
  130.9 7.7 %collective-permute-done.23.refs_3_ = bf16[136,1152]{1,0:T(8,128)(2,1)S(1)} collective-permute-done((bf16[136,1152]{1,0:T(8,128)(2,1)S(1)}, bf16[136,1152]{1,0:T(8,128)(2,1)S(1)}, u32[]{:S(2)}, u32[]{:S(2)}) %collective-permute-start.23) | collective-permute-done | bytes 313376 | tf_op jit(solution)/shard_map/ppermute | solution.py:704
  138.6 5.6 %collective-permute-done.22.refs_2_ = bf16[136,1152]{1,0:T(8,128)(2,1)S(1)} collective-permute-done((bf16[136,1152]{1,0:T(8,128)(2,1)S(1)}, bf16[136,1152]{1,0:T(8,128)(2,1)S(1)}, u32[]{:S(2)}, u32[]{:S(2)}) %collective-permute-start.22) | collective-permute-done | bytes 313376 | tf_op jit(solution)/shard_map/ppermute | solution.py:704
  148.7 5.0 %mlp.2 = (bf16[2,272,576]{2,1,0:T(8,128)(2,1)S(1)}, bf16[2,272,576]{2,1,0:T(8,128)(2,1)S(1)}, f32[1,576]{1,0:T(1,128)S(1)}, bf16[4,136,1152]{2,1,0:T(8,128)(2,1)S(1)}, f32[8,128]{1,0:T(8,128)S(1)}) custom-call(bf16[2,272,1152]{2,1,0:T(8,128)(2,1)} %bitcast.19.refs_0_.refs_1_, bf16[2,272,1152]{2,1,0:T(8,128)(2,1)S(1)} %bitcast.61, ...), custom_call_target="tpu_custom_call" | custom-call | flops 100000000 | bytes 1000 | tf_op jit(solution)/shard_map/mlp/pallas_call | solution.py:53
  153.9 18.0 %mlp.3 = (bf16[2,272,576]{2,1,0:T(8,128)(2,1)S(1)}, bf16[2,272,576]{2,1,0:T(8,128)(2,1)S(1)}, f32[1,576]{1,0:T(1,128)S(1)}, f32[4,136,1152]{2,1,0:T(8,128)S(1)}, f32[8,128]{1,0:T(8,128)S(1)}) custom-call(bf16[2,272,1152]{2,1,0:T(8,128)(2,1)} %bitcast.15.refs_0_, bf16[2,272,1152]{2,1,0:T(8,128)(2,1)S(1)} %bitcast.58, bf16[1152,576]{1,0:T(8,128)(2,1)S(1)} %bitcast.49, ...), custom_call_target="tpu_custom_call" | custom-call | flops 100000000 | bytes 1000 | tf_op jit(solution)/shard_map/mlp/pallas_call | solution.py:53
  176.8 8.3 %grad_mlp.1 = (bf16[4,4,72,1152]{3,2,1,0:T(8,128)(2,1)S(1)}, f32[8,128]{1,0:T(8,128)S(1)}) custom-call(bf16[2,272,1152]{2,1,0:T(8,128)(2,1)} %bitcast.15.refs_0_, bf16[2,272,1152]{2,1,0:T(8,128)(2,1)} %bitcast.19.refs_0_.refs_1_, bf16[2,272,576]{2,1,0:T(8,128)(2,1)S(1)} %get-tuple-element.217.refs_2_, bf16[2,272,576]{2,1,0:T(8,128)(2,1)S(1)} %get-tuple-element.218.refs_3_, ...), custom_call_target="tpu_custom_call" | custom-call | flops 20000000000 | bytes 1000 | tf_op jit(solution)/shard_map/grad_mlp/pallas_call | solution.py:53
  202.9 5.2 %collective-permute-done.33.refs_3_ = bf16[136,1152]{1,0:T(8,128)(2,1)S(1)} collective-permute-done((bf16[136,1152]{1,0:T(8,128)(2,1)S(1)}, bf16[136,1152]{1,0:T(8,128)(2,1)S(1)}, u32[]{:S(2)}, u32[]{:S(2)}) %collective-permute-start.33) | collective-permute-done | bytes 313376 | tf_op jit(solution)/shard_map/ppermute | solution.py:704
  208.0 4.8 %collective-permute-done.32.refs_2_ = bf16[136,1152]{1,0:T(8,128)(2,1)S(1)} collective-permute-done((bf16[136,1152]{1,0:T(8,128)(2,1)S(1)}, bf16[136,1152]{1,0:T(8,128)(2,1)S(1)}, u32[]{:S(2)}, u32[]{:S(2)}) %collective-permute-start.32) | collective-permute-done | bytes 313376 | tf_op jit(solution)/shard_map/ppermute | solution.py:704
  232.1 5.9 %collective-permute-done.36.refs_5_ = bf16[136,1152]{1,0:T(8,128)(2,1)S(1)} collective-permute-done((bf16[136,1152]{1,0:T(8,128)(2,1)S(1)}, bf16[136,1152]{1,0:T(8,128)(2,1)S(1)}, u32[]{:S(2)}, u32[]{:S(2)}) %collective-permute-start.36) | collective-permute-done | bytes 313376 | tf_op jit(solution)/shard_map/ppermute | solution.py:704
  243.8 5.0 %grad_attend.1 = (bf16[4,4,72,896]{3,2,1,0:T(8,128)(2,1)S(1)}, f32[8,128]{1,0:T(8,128)S(1)}) custom-call(bf16[2,272,1152]{2,1,0:T(8,128)(2,1)S(1)} %bitcast.66, bf16[2,272,1152]{2,1,0:T(8,128)(2,1)} %bitcast.14.refs_0_.refs_1_, bf16[2,272,512]{2,1,0:T(8,128)(2,1)S(1)} %get-tuple-element.246.refs_2_, bf16[2,272,512]{2,1,0:T(8,128)(2,1)S(1)} %get-tuple-element.247.refs_3_, ...), custom_call_target="tpu_custom_call" | custom-call | flops 20000000000 | bytes 1000 | tf_op jit(solution)/shard_map/grad_attend/pallas_call | solution.py:53
  252.4 4.7 %collective-permute-done.41.refs_4_ = bf16[136,1152]{1,0:T(8,128)(2,1)} collective-permute-done((bf16[136,1152]{1,0:T(8,128)(2,1)}, bf16[136,1152]{1,0:T(8,128)(2,1)}, u32[]{:S(2)}, u32[]{:S(2)}) %collective-permute-start.41) | collective-permute-done | bytes 313376 | tf_op jit(solution)/shard_map/ppermute | solution.py:704
  263.6 6.8 %collective-permute-done.44.refs_3_ = bf16[136,1152]{1,0:T(8,128)(2,1)S(1)} collective-permute-done((bf16[136,1152]{1,0:T(8,128)(2,1)S(1)}, bf16[136,1152]{1,0:T(8,128)(2,1)S(1)}, u32[]{:S(2)}, u32[]{:S(2)}) %collective-permute-start.44) | collective-permute-done | bytes 313376 | tf_op jit(solution)/shard_map/ppermute | solution.py:704
  297.8 14.7 %collective-permute-done.46.refs_1_ = bf16[2,72,1152]{2,1,0:T(8,128)(2,1)S(1)} collective-permute-done((bf16[2,72,1152]{2,1,0:T(8,128)(2,1)S(1)}, bf16[2,72,1152]{2,1,0:T(8,128)(2,1)S(1)}, u32[]{:S(2)}, u32[]{:S(2)}) %collective-permute-start.46) | collective-permute-done | bytes 331808 | tf_op jit(solution)/shard_map/ppermute | solution.py:704
  322.6 6.1 %all-to-all-done.3.refs_0_ = bf16[8,72,512]{2,1,0:T(8,128)(2,1)S(1)} async-done(((bf16[8,72,512]{2,1,0:T(8,128)(2,1)}), bf16[8,72,512]{2,1,0:T(8,128)(2,1)S(1)}, u32[]{:S(2)}, u32[]{:S(2)}) %all-to-all-start.3) | async-done | bytes 589856 | tf_op jit(solution)/shard_map/all_to_all | solution.py:881
  330.1 6.1 %collective-permute-done.48.refs_1_ = bf16[72,1152]{1,0:T(8,128)(2,1)S(1)} collective-permute-done((bf16[72,1152]{1,0:T(8,128)(2,1)S(1)}, bf16[72,1152]{1,0:T(8,128)(2,1)S(1)}, u32[]{:S(2)}, u32[]{:S(2)}) %collective-permute-start.48) | collective-permute-done | bytes 165920 | tf_op jit(solution)/shard_map/ppermute | solution.py:704
  (287 shorter events, 166.2 us)
Async XLA Ops:
  16.6 15.6 %collective-permute-start.1 = (bf16[80,1152]{1,0:T(8,128)(2,1)S(1)}, bf16[80,1152]{1,0:T(8,128)(2,1)S(1)}, u32[]{:S(2)}, u32[]{:S(2)}) collective-permute-start(bf16[80,1152]{1,0:T(8,128)(2,1)S(1)} %get-tuple-element.153.refs_0_), channel_id=1, source_target_pairs={{0,16},{8,24},{16,0},{24,8},{1,17},{9,25},{17,1},{25,9},{2,18},{10... | collective-permute-start | bytes 552968 | tf_op jit(solution)/shard_map/ppermute | solution.py:725
  16.6 15.6 %collective-permute-start = (bf16[80,1152]{1,0:T(8,128)(2,1)S(1)}, bf16[80,1152]{1,0:T(8,128)(2,1)S(1)}, u32[]{:S(2)}, u32[]{:S(2)}) collective-permute-start(bf16[80,1152]{1,0:T(8,128)(2,1)S(1)} %get-tuple-element.153.refs_0_), channel_id=1, source_target_pairs={{0,8},{8,16},{16,24},{24,0},{1,9},{9,17},{17,25},{25,1},{2,10},{10... | collective-permute-start | bytes 552968 | tf_op jit(solution)/shard_map/ppermute | solution.py:725
  17.6 24.0 %all-to-all-start = ((bf16[8,136,288]{2,1,0:T(8,128)(2,1)}), bf16[8,136,288]{2,1,0:T(8,128)(2,1)S(1)}, u32[]{:S(2)}, u32[]{:S(2)}) async-start(bf16[8,136,288]{2,1,0:T(8,128)(2,1)} %get-tuple-element.151), calls=%async_computation | async-start | bytes 1671168 | tf_op jit(solution)/shard_map/all_to_all | solution.py:782
  21.4 65.2 %all-gather.5.cloned.1.call-start = ((), (), s32[]{:S(2)}) async-start(), calls=%async_computation.10 | async-start | bytes 2580480 | tf_op jit(solution)/shard_map/all_gather | solution.py:735
  24.6 15.7 %collective-permute-start.5 = (bf16[72,1088]{1,0:T(8,128)(2,1)S(1)}, bf16[72,1088]{1,0:T(8,128)(2,1)S(1)}, u32[]{:S(2)}, u32[]{:S(2)}) collective-permute-start(bf16[72,1088]{1,0:T(8,128)(2,1)S(1)} %get-tuple-element.161), channel_id=1, source_target_pairs={{0,6},{2,4},{4,2},{6,0},{1,7},{3,5},{5,3},{7,1},{8,14},{10,12},{12... | collective-permute-start | bytes 470024 | tf_op jit(solution)/shard_map/ppermute | solution.py:704
  41.6 103.7 %all-gather.7.cloned.1.call-start = ((), (), s32[]{:S(2)}) async-start(), calls=%async_computation.11 | async-start | bytes 3317760 | tf_op jit(solution)/shard_map/all_gather | solution.py:735
  48.0 15.5 %collective-permute-start.9 = (bf16[136,1152]{1,0:T(8,128)(2,1)S(1)}, bf16[136,1152]{1,0:T(8,128)(2,1)S(1)}, u32[]{:S(2)}, u32[]{:S(2)}) collective-permute-start(bf16[136,1152]{1,0:T(8,128)(2,1)S(1)} %get-tuple-element.170), channel_id=1, source_target_pairs={{0,5},{1,4},{4,1},{5,0},{2,7},{3,6},{6,3},{7,2},{8,13},{9,12},{12,... | collective-permute-start | bytes 940040 | tf_op jit(solution)/shard_map/ppermute | solution.py:704
  65.5 14.8 %collective-permute-start.11 = (bf16[136,1152]{1,0:T(8,128)(2,1)S(1)}, bf16[136,1152]{1,0:T(8,128)(2,1)S(1)}, u32[]{:S(2)}, u32[]{:S(2)}) collective-permute-start(bf16[136,1152]{1,0:T(8,128)(2,1)S(1)} %get-tuple-element.177.refs_0_), channel_id=1, source_target_pairs={{0,4},{4,0},{1,5},{5,1},{2,6},{6,2},{3,7},{7,3},{8,12},{12,8},{9,1... | collective-permute-start | bytes 940040 | tf_op jit(solution)/shard_map/ppermute | solution.py:704
  80.5 169.6 %reduce-scatter.4.cloned.1.call-start = ((), (), s32[]{:S(2)}) async-start(), calls=%async_computation.7 | async-start | bytes 3317760 | tf_op jit(solution)/shard_map/reduce_scatter | solution.py:878
  97.6 15.5 %collective-permute-start.19 = (bf16[136,1152]{1,0:T(8,128)(2,1)S(1)}, bf16[136,1152]{1,0:T(8,128)(2,1)S(1)}, u32[]{:S(2)}, u32[]{:S(2)}) collective-permute-start(bf16[136,1152]{1,0:T(8,128)(2,1)S(1)} %get-tuple-element.193.refs_0_), channel_id=1, source_target_pairs={{0,4},{4,0},{1,5},{5,1},{2,6},{6,2},{3,7},{7,3},{8,12},{12,8},{9,1... | collective-permute-start | bytes 940040 | tf_op jit(solution)/shard_map/ppermute | solution.py:704
  98.1 14.9 %collective-permute-start.18 = (bf16[136,1152]{1,0:T(8,128)(2,1)S(1)}, bf16[136,1152]{1,0:T(8,128)(2,1)S(1)}, u32[]{:S(2)}, u32[]{:S(2)}) collective-permute-start(bf16[136,1152]{1,0:T(8,128)(2,1)S(1)} %get-tuple-element.193.refs_0_), channel_id=1, source_target_pairs={{0,1},{1,0},{2,3},{3,2},{4,5},{5,4},{6,7},{7,6},{8,9},{9,8},{10,11... | collective-permute-start | bytes 940040 | tf_op jit(solution)/shard_map/ppermute | solution.py:704
  103.9 15.8 %collective-permute-start.15 = (bf16[136,1152]{1,0:T(8,128)(2,1)S(1)}, bf16[136,1152]{1,0:T(8,128)(2,1)S(1)}, u32[]{:S(2)}, u32[]{:S(2)}) collective-permute-start(bf16[136,1152]{1,0:T(8,128)(2,1)S(1)} %get-tuple-element.189), channel_id=1, source_target_pairs={{0,1},{1,0},{2,3},{3,2},{4,5},{5,4},{6,7},{7,6},{8,9},{9,8},{10,11... | collective-permute-start | bytes 940040 | tf_op jit(solution)/shard_map/ppermute | solution.py:704
  106.9 19.2 %collective-permute-start.17 = (bf16[136,1152]{1,0:T(8,128)(2,1)S(1)}, bf16[136,1152]{1,0:T(8,128)(2,1)S(1)}, u32[]{:S(2)}, u32[]{:S(2)}) collective-permute-start(bf16[136,1152]{1,0:T(8,128)(2,1)S(1)} %get-tuple-element.191), channel_id=1, source_target_pairs={{0,5},{1,4},{4,1},{5,0},{2,7},{3,6},{6,3},{7,2},{8,13},{9,12},{12,... | collective-permute-start | bytes 940040 | tf_op jit(solution)/shard_map/ppermute | solution.py:704
  130.9 16.6 %collective-permute-start.25 = (bf16[4,136,1152]{2,1,0:T(8,128)(2,1)S(1)}, bf16[4,136,1152]{2,1,0:T(8,128)(2,1)S(1)}, u32[]{:S(2)}, u32[]{:S(2)}) collective-permute-start(bf16[4,136,1152]{2,1,0:T(8,128)(2,1)S(1)} %get-tuple-element.200), channel_id=1, source_target_pairs={{0,2},{2,0},{1,3},{3,1},{4,6},{6,4},{5,7},{7,5},{8,10},{10,8},{9,1... | collective-permute-start | bytes 3760136 | tf_op jit(solution)/shard_map/ppermute | solution.py:704
  153.7 18.2 %collective-permute-start.26 = (bf16[4,136,1152]{2,1,0:T(8,128)(2,1)S(1)}, bf16[4,136,1152]{2,1,0:T(8,128)(2,1)S(1)}, u32[]{:S(2)}, u32[]{:S(2)}) collective-permute-start(bf16[4,136,1152]{2,1,0:T(8,128)(2,1)S(1)} %get-tuple-element.211), channel_id=1, source_target_pairs={{0,2},{2,0},{1,3},{3,1},{4,6},{6,4},{5,7},{7,5},{8,10},{10,8},{9,1... | collective-permute-start | bytes 3760136 | tf_op jit(solution)/shard_map/ppermute | solution.py:704
  176.2 15.0 %collective-permute-start.29 = (bf16[136,1152]{1,0:T(8,128)(2,1)}, bf16[136,1152]{1,0:T(8,128)(2,1)}, u32[]{:S(2)}, u32[]{:S(2)}) collective-permute-start(bf16[136,1152]{1,0:T(8,128)(2,1)} %get-tuple-element.215), channel_id=1, source_target_pairs={{0,5},{1,4},{4,1},{5,0},{2,7},{3,6},{6,3},{7,2},{8,13},{9,12},{12,... | collective-permute-start | bytes 940040 | tf_op jit(solution)/shard_map/ppermute | solution.py:704
  186.7 127.1 %reduce-scatter.6.cloned.1.call-start = ((), (), s32[]{:S(2)}) async-start(), calls=%async_computation.8 | async-start | bytes 2580480 | tf_op jit(solution)/shard_map/reduce_scatter | solution.py:878
  220.2 18.8 %collective-permute-start.38 = (bf16[4,136,1152]{2,1,0:T(8,128)(2,1)S(1)}, bf16[4,136,1152]{2,1,0:T(8,128)(2,1)S(1)}, u32[]{:S(2)}, u32[]{:S(2)}) collective-permute-start(bf16[4,136,1152]{2,1,0:T(8,128)(2,1)S(1)} %get-tuple-element.239), channel_id=1, source_target_pairs={{0,2},{2,0},{1,3},{3,1},{4,6},{6,4},{5,7},{7,5},{8,10},{10,8},{9,1... | collective-permute-start | bytes 3760136 | tf_op jit(solution)/shard_map/ppermute | solution.py:704
  274.4 15.4 %all-to-all-start.2 = ((bf16[8,72,576]{2,1,0:T(8,128)(2,1)}), bf16[8,72,576]{2,1,0:T(8,128)(2,1)}, u32[]{:S(2)}, u32[]{:S(2)}) async-start(bf16[8,72,576]{2,1,0:T(8,128)(2,1)} %get-tuple-element.266), calls=%async_computation.4 | async-start | bytes 1474560 | tf_op jit(solution)/shard_map/all_to_all | solution.py:881
  278.6 40.7 %reduce-scatter.8.cloned.1.call-start = ((), (), s32[]{:S(2)}) async-start(), calls=%async_computation.9 | async-start | bytes 921600 | tf_op jit(solution)/shard_map/reduce_scatter | solution.py:878
  289.8 25.9 %all-to-all-start.1 = ((bf16[8,136,288]{2,1,0:T(8,128)(2,1)}), bf16[8,136,288]{2,1,0:T(8,128)(2,1)S(1)}, u32[]{:S(2)}, u32[]{:S(2)}) async-start(bf16[8,136,288]{2,1,0:T(8,128)(2,1)} %copy-done.23), calls=%async_computation.2 | async-start | bytes 1671168 | tf_op jit(solution)/shard_map/all_to_all | solution.py:964
  293.4 19.2 %collective-permute-start.46 = (bf16[2,72,1152]{2,1,0:T(8,128)(2,1)S(1)}, bf16[2,72,1152]{2,1,0:T(8,128)(2,1)S(1)}, u32[]{:S(2)}, u32[]{:S(2)}) collective-permute-start(bf16[2,72,1152]{2,1,0:T(8,128)(2,1)S(1)} %get-tuple-element.265.refs_0_), channel_id=1, source_target_pairs={{0,1},{1,0},{2,3},{3,2},{4,5},{5,4},{6,7},{7,6},{8,9},{9,8},{10,11... | collective-permute-start | bytes 995336 | tf_op jit(solution)/shard_map/ppermute | solution.py:704
  319.3 17.7 %collective-permute-start.47 = (bf16[80,1152]{1,0:T(8,128)(2,1)}, bf16[80,1152]{1,0:T(8,128)(2,1)S(1)}, u32[]{:S(2)}, u32[]{:S(2)}) collective-permute-start(bf16[80,1152]{1,0:T(8,128)(2,1)} %reduce-scatter.8.cloned.1.call-done.refs_0_), channel_id=1, source_target_pairs={{0,1},{1,0},{2,3},{3,2},{4,5},{5,4},{6,7},{7,6},{8,9},{9,8},{10,11... | collective-permute-start | bytes 552968 | tf_op jit(solution)/shard_map/ppermute | solution.py:704
  321.2 15.0 %collective-permute-start.48 = (bf16[72,1152]{1,0:T(8,128)(2,1)S(1)}, bf16[72,1152]{1,0:T(8,128)(2,1)S(1)}, u32[]{:S(2)}, u32[]{:S(2)}) collective-permute-start(bf16[72,1152]{1,0:T(8,128)(2,1)S(1)} %get-tuple-element.274.refs_0_), channel_id=1, source_target_pairs={{0,1},{1,0},{2,3},{3,2},{4,5},{5,4},{6,7},{7,6},{8,9},{9,8},{10,11... | collective-permute-start | bytes 497672 | tf_op jit(solution)/shard_map/ppermute | solution.py:704
  (104 other events, 783.8 us)
Sparse Core Ops, SparseCore 0:
  41.7 44.7 all-gather.4
  88.7 54.0 all-gather.6
  186.8 51.2 reduce-scatter.3
  250.2 41.7 reduce-scatter.5
  294.3 22.2 reduce-scatter.7
